TPU v7x, 32 devices: a whole 2x2x4 slice. The times are simulated.
32 devices in a mesh: comp: 8 (over y, x, core), band: 4 (over z).
Axes of the slice: x: 2, y: 2, z: 4, core: 2. Of those that a mesh axis runs over, the one named last changes fastest.
Arguments:
- spectrum: float32 [1152, 96, 256], P('comp', 'band'), as said below
- wet_mask: int32 [96, 256], P('band'), may hold values 0 or 1
- quad_matrix: bfloat16 [1152, 1152], replicated, may hold values from -0.1875 to 0.1875
- dissipation: float32 [1152], replicated, may hold values from 0.2 to 2
- circulation: float32 [3, 32, 1024], P(None, 'band', 'comp'), may hold values from -3 to 3
- source_points: int32 [3, 32, 1024], P(None, 'band', 'comp'), may hold values from 0 to 6143
Outputs:
- spectrum_out: float32 [1152, 96, 256], P('comp', 'band')
- circulation_out: float32 [3, 32, 1024], P(None, 'band', 'comp')
Inputs may be any that keep to these rules, and one draw needn't show every extreme that they name: `spectrum`: every entry is positive. `source_points`: each entry numbers a wave point of the band that holds the cell's row, row by row within the band.
All inputs are finite; a program needn't handle non-finite values. No bound on the sum of `wet_mask` on one device may be relied on, other than what follows from the above.
Results may differ from a plain program's by a relative error of at most 0.007.
Values may be sent and summed in bfloat16 or wider, within the bound.
A program may use at most 128 MiB of HBM per device.

v0:
```python
import math

import jax
import jax.numpy as jnp
from jax import lax
from jax.sharding import PartitionSpec as P

NF = 36
ND = 32
SUBSTEPS = 4
SRC_STEPS = 4
SW_STEPS = 8


step_source = 0.1
wave_speed = 0.35
friction = 0.05
forcing_gain = 0.15


def extended_2(cells, sides, width):
    for axis, dim in sides:
        count = lax.axis_size(axis)
        ends = count - 1
        head = lax.slice_in_dim(cells, 0, width, axis=dim)
        tail = lax.slice_in_dim(cells, cells.shape[dim] - width, cells.shape[dim], axis=dim)
        cells = jnp.concatenate(
            [
                lax.ppermute(tail, axis, [(i, (i + 1) % count) for i in range(ends)]),
                cells,
                lax.ppermute(head, axis, [((i + 1) % count, i) for i in range(ends)]),
            ],
            axis=dim,
        )
    return cells


def component_tables(offset, local_count, freqs, headings):
    indices = offset + jnp.arange(local_count, dtype=jnp.int32)
    frequency = (indices // headings).astype(jnp.float32)
    heading = (indices % headings).astype(jnp.float32)
    heading_angle = 2.0 * math.pi * (heading + 0.5) / headings
    fraction = (frequency + 0.5) / freqs
    group_speed = 0.25 + 0.4 * fraction
    wave_ratio = 0.5 + 0.5 * fraction
    cosine = jnp.cos(heading_angle)
    sine_part = jnp.sin(heading_angle)
    speed_east = group_speed * cosine
    speed_north = group_speed * sine_part
    stress_coef = jnp.stack(
        [
            wave_ratio * (1.0 + cosine * cosine) - 0.5,
            wave_ratio * sine_part * cosine,
            wave_ratio * (1.0 + sine_part * sine_part) - 0.5,
        ]
    )
    return (speed_east, speed_north, stress_coef)


def upwind(extended, speed_east, speed_north, wet_rows):
    middle = extended[:, 1:-1, :]
    west_cells = extended[:, :-2, :]
    east_cells = extended[:, 2:, :]
    padded = jnp.pad(middle, ((0, 0), (0, 0), (1, 1)))
    south_cells = padded[:, :, :-2]
    north_cells = padded[:, :, 2:]
    along_rows = speed_east[:, None, None]
    along_cols = speed_north[:, None, None]
    flux_rows = jnp.maximum(along_rows, 0.0) * (middle - west_cells) + jnp.minimum(
        along_rows, 0.0
    ) * (east_cells - middle)
    flux_cols = jnp.maximum(along_cols, 0.0) * (middle - south_cells) + jnp.minimum(
        along_cols, 0.0
    ) * (north_cells - middle)
    return (middle - flux_rows - flux_cols) * wet_rows


def sources(base, quad_matrix, dissipation):
    current = base
    for repeat in range(SRC_STEPS):
        product = jnp.dot(
            quad_matrix, current.astype(jnp.bfloat16), preferred_element_type=jnp.float32
        )
        energy_level = jnp.mean(current, axis=0, keepdims=True)
        current = current + step_source * current * (product - dissipation[:, None] * energy_level)
    return current


def diff_rows(extended):
    return 0.5 * (extended[2:, 1:-1] - extended[:-2, 1:-1])


def diff_cols(extended):
    return 0.5 * (extended[1:-1, 2:] - extended[1:-1, :-2])


def on_device(spectrum, wet_mask, quad_matrix, dissipation, circulation, source_points):
    local_count = spectrum.shape[0]
    row_count = spectrum.shape[1]
    columns = spectrum.shape[2]
    groups = lax.axis_size("comp")
    component_total = local_count * groups
    offset = lax.axis_index("comp") * local_count
    speed_east, speed_north, stress_coef = component_tables(offset, local_count, NF, ND)
    wetness = wet_mask.astype(jnp.float32)[None]
    density = spectrum
    for substep in range(SUBSTEPS):
        extended = extended_2(density, (("band", 1),), 1)
        density = upwind(extended, speed_east, speed_north, wetness)
    sent_block = lax.optimization_barrier(density.astype(jnp.bfloat16)).reshape(
        local_count, groups, -1
    )
    base = lax.all_to_all(sent_block, "comp", split_axis=1, concat_axis=0, tiled=True)[
        :, 0, :
    ].astype(jnp.float32)
    current = sources(base, quad_matrix, dissipation)
    increment = (current - base).astype(jnp.bfloat16)
    returned = lax.all_to_all(
        increment[:, None, :], "comp", split_axis=0, concat_axis=1, tiled=True
    )
    increment_back = returned.reshape(local_count, row_count, columns).astype(jnp.float32)
    coupled = sent_block.reshape(local_count, -1).astype(jnp.float32) + increment_back.reshape(
        local_count, -1
    )
    partial_value = jnp.dot(stress_coef, coupled, precision=lax.Precision.HIGHEST) / component_total
    band_stress = lax.psum(partial_value.astype(jnp.bfloat16), "comp").astype(jnp.float32)
    new_spectrum = density + increment_back
    tile_rows = circulation.shape[1]
    tile_cols = circulation.shape[2]
    picked = jnp.take(band_stress, source_points.reshape(-1), axis=1).reshape(
        3, 3, tile_rows, tile_cols
    )
    cell_stress = 0.5 * picked[:, 0] + 0.3 * picked[:, 1] + 0.2 * picked[:, 2]
    margin_cols = 2 * SW_STEPS + 1
    whole_state, whole_stress = (
        lax.all_gather(circulation, "band", axis=1, tiled=True),
        lax.all_gather(cell_stress, "band", axis=1, tiled=True),
    )
    wide_state, wide_stress = (
        extended_2(whole_state, (("comp", 2),), margin_cols),
        extended_2(whole_stress, (("comp", 2),), margin_cols),
    )
    wide_cols = wide_state.shape[2]
    global_col = (
        lax.axis_index("comp") * tile_cols - margin_cols + jnp.arange(wide_cols, dtype=jnp.int32)
    )
    inside = ((global_col >= 0) & (global_col < tile_cols * groups)).astype(jnp.float32)[None, :]
    rimmed = jnp.pad(wide_stress, ((0, 0), (1, 1), (1, 1)))
    force_down = -(diff_rows(rimmed[0]) + diff_cols(rimmed[1]))
    force_across = -(diff_rows(rimmed[1]) + diff_cols(rimmed[2]))
    height = wide_state[0]
    flow_down = wide_state[1]
    flow_across = wide_state[2]
    for repeat in range(SW_STEPS):
        down_ext = jnp.pad(flow_down, 1)
        across_ext = jnp.pad(flow_across, 1)
        height = (height - wave_speed * (diff_rows(down_ext) + diff_cols(across_ext))) * inside
        height_ext = jnp.pad(height, 1)
        flow_down = (
            (1.0 - friction) * flow_down
            - wave_speed * diff_rows(height_ext)
            + forcing_gain * force_down
        ) * inside
        flow_across = (
            (1.0 - friction) * flow_across
            - wave_speed * diff_cols(height_ext)
            + forcing_gain * force_across
        ) * inside
    stacked = jnp.stack([height, flow_down, flow_across])
    row_start = lax.axis_index("band") * tile_rows
    own_rows = lax.dynamic_slice_in_dim(stacked, row_start, tile_rows, 1)
    return (new_spectrum, own_rows[:, :, margin_cols : margin_cols + tile_cols])


def solution(mesh):
    in_specs = (
        P("comp", "band", None),
        P("band", None),
        P(),
        P(),
        P(None, "band", "comp"),
        P(None, "band", "comp"),
    )
    out_specs = (P("comp", "band", None), P(None, "band", "comp"))
    return jax.shard_map(
        on_device, mesh=mesh, in_specs=in_specs, out_specs=out_specs, check_vma=False
    )
```

profile of v0, /device:TPU:0, one launch (start us, length us, event | category | flops | bytes accessed | tf_op | source)
XLA Modules:
  0.0 251.7 jit_solution(9581149774138953898)
XLA Ops:
  0.6 2.0 fusion.237
  2.6 4.9 %collective-permute-start = (f32[144,1,256]{2,1,0:T(1,128)S(1)}, f32[144,1,256]{2,1,0:T(1,128)S(1)}, u32[]{:S(2)}, u32[]{:S(2)}) collective-permute-start(f32[144,1,256]{2,1,0:T(1,128)S(1)} %get-tuple-element.14), channel_id=1, source_target_pairs={{0,1},{1,2},{2,3},{4,5},{5,6},{6,7},{8,9},{9,10},{10,11},{12,13},{... | collective-permute-start | bytes 442376 | tf_op jit(solution)/shard_map/ppermute | solution.py:29
  7.6 1.3 collective-permute-start.1
  8.9 0.7 convert_element_type.164
  9.8 0.9 collective-permute-done
  10.7 4.1 %collective-permute-done.1 = f32[144,1,256]{2,1,0:T(1,128)S(1)} collective-permute-done((f32[144,1,256]{2,1,0:T(1,128)S(1)}, f32[144,1,256]{2,1,0:T(1,128)S(1)}, u32[]{:S(2)}, u32[]{:S(2)}) %collective-permute-start.1) | collective-permute-done | bytes 147488 | tf_op jit(solution)/shard_map/ppermute | solution.py:31
  14.8 11.0 %fusion.16 = f32[144,24,256]{2,1,0:T(8,128)S(1)} fusion(f32[144,24,256]{2,1,0:T(8,128)} %param.6, f32[144,1,256]{2,1,0:T(1,128)S(1)} %collective-permute-done.1, f32[144,1,256]{2,1,0:T(1,128)S(1)} %collective-permute-done, f32[24,256]{1,0:T(8,128)S(1)} %convert_element_type.164, f32[144]{0:T(256)S(1)} %get-tuple-element.49, f32[144]{0:T(256)S(1)} %get-tuple-element.50, ...), kind=kLoop, calls=%fused_computation.33 | loop fusion | flops 13271040 | bytes 7399680 | tf_op jit(solution)/shard_map/mul | solution.py:75
  25.8 0.2 fusion.236
  26.0 3.5 %collective-permute-start.2 = (f32[144,1,256]{2,1,0:T(1,128)S(1)}, f32[144,1,256]{2,1,0:T(1,128)S(1)}, u32[]{:S(2)}, u32[]{:S(2)}) collective-permute-start(f32[144,1,256]{2,1,0:T(1,128)S(1)} %get-tuple-element.12), channel_id=1, source_target_pairs={{0,1},{1,2},{2,3},{4,5},{5,6},{6,7},{8,9},{9,10},{10,11},{12,13},{... | collective-permute-start | bytes 442376 | tf_op jit(solution)/shard_map/ppermute | solution.py:29
  29.5 1.3 collective-permute-start.3
  30.8 1.3 collective-permute-done.2
  32.2 4.4 %collective-permute-done.3 = f32[144,1,256]{2,1,0:T(1,128)S(1)} collective-permute-done((f32[144,1,256]{2,1,0:T(1,128)S(1)}, f32[144,1,256]{2,1,0:T(1,128)S(1)}, u32[]{:S(2)}, u32[]{:S(2)}) %collective-permute-start.3) | collective-permute-done | bytes 147488 | tf_op jit(solution)/shard_map/ppermute | solution.py:31
  36.6 4.6 %fusion.23 = f32[144,24,256]{2,1,0:T(8,128)S(1)} fusion(f32[144,24,256]{2,1,0:T(8,128)S(1)} %fusion.16, f32[144,1,256]{2,1,0:T(1,128)S(1)} %collective-permute-done.3, f32[144,1,256]{2,1,0:T(1,128)S(1)} %collective-permute-done.2, f32[24,256]{1,0:T(8,128)S(1)} %convert_element_type.164, f32[144]{0:T(256)S(1)} %get-tuple-element.49, ...), kind=kLoop, calls=%fused_computation.40 | loop fusion | flops 13271040 | bytes 7399680 | tf_op jit(solution)/shard_map/mul | solution.py:75
  41.2 0.2 fusion.235
  41.4 3.5 %collective-permute-start.4 = (f32[144,1,256]{2,1,0:T(1,128)S(1)}, f32[144,1,256]{2,1,0:T(1,128)S(1)}, u32[]{:S(2)}, u32[]{:S(2)}) collective-permute-start(f32[144,1,256]{2,1,0:T(1,128)S(1)} %get-tuple-element.10), channel_id=1, source_target_pairs={{0,1},{1,2},{2,3},{4,5},{5,6},{6,7},{8,9},{9,10},{10,11},{12,13},{... | collective-permute-start | bytes 442376 | tf_op jit(solution)/shard_map/ppermute | solution.py:29
  44.9 1.3 collective-permute-start.5
  46.2 1.3 collective-permute-done.4
  47.6 4.4 %collective-permute-done.5 = f32[144,1,256]{2,1,0:T(1,128)S(1)} collective-permute-done((f32[144,1,256]{2,1,0:T(1,128)S(1)}, f32[144,1,256]{2,1,0:T(1,128)S(1)}, u32[]{:S(2)}, u32[]{:S(2)}) %collective-permute-start.5) | collective-permute-done | bytes 147488 | tf_op jit(solution)/shard_map/ppermute | solution.py:31
  51.9 4.6 %fusion.30 = f32[144,24,256]{2,1,0:T(8,128)S(1)} fusion(f32[144,24,256]{2,1,0:T(8,128)S(1)} %fusion.23, f32[144,1,256]{2,1,0:T(1,128)S(1)} %collective-permute-done.5, f32[144,1,256]{2,1,0:T(1,128)S(1)} %collective-permute-done.4, f32[24,256]{1,0:T(8,128)S(1)} %convert_element_type.164, f32[144]{0:T(256)S(1)} %get-tuple-element.49, ...), kind=kLoop, calls=%fused_computation.47 | loop fusion | flops 13271040 | bytes 7399680 | tf_op jit(solution)/shard_map/mul | solution.py:75
  56.6 0.2 fusion.234
  56.8 1.9 collective-permute-start.6
  58.7 1.3 collective-permute-start.7
  60.0 1.3 collective-permute-done.6
  61.4 4.4 %collective-permute-done.7 = f32[144,1,256]{2,1,0:T(1,128)S(1)} collective-permute-done((f32[144,1,256]{2,1,0:T(1,128)S(1)}, f32[144,1,256]{2,1,0:T(1,128)S(1)}, u32[]{:S(2)}, u32[]{:S(2)}) %collective-permute-start.7) | collective-permute-done | bytes 147488 | tf_op jit(solution)/shard_map/ppermute | solution.py:31
  65.8 6.0 %fusion.232 = (bf16[144,24,256]{2,1,0:T(8,128)(2,1)}, f32[144,24,256]{2,1,0:T(8,128)}) fusion(f32[24,256]{1,0:T(8,128)S(1)} %convert_element_type.164, f32[144,24,256]{2,1,0:T(8,128)S(1)} %fusion.30, f32[144]{0:T(256)S(1)} %get-tuple-element.49, f32[144]{0:T(256)S(1)} %get-tuple-element.50, f32[144,1,256]{2,1,0:T(1,128)S(1)} %collective-permute-done.7, ...), kind=kLoop, calls=%fused_computation.378 | loop fusion | flops 14155776 | bytes 9169152 | tf_op jit(solution)/shard_map/convert_element_type | solution.py:110
  71.7 3.8 %reshape.284 = bf16[144,8,768]{2,1,0:T(8,128)(2,1)} reshape(bf16[144,24,256]{2,1,0:T(8,128)(2,1)} %get-tuple-element.6) | data formatting | bytes 3538944 | tf_op jit(solution)/shard_map/reshape | solution.py:110
  75.6 3.1 %copy.24 = bf16[144,8,768]{2,0,1:T(8,128)(2,1)} copy(bf16[144,8,768]{2,1,0:T(8,128)(2,1)} %reshape.284) | data formatting | bytes 3538944 | tf_op jit(solution)/shard_map/reshape | solution.py:110
  78.6 4.3 %all-to-all-start = ((bf16[144,8,768]{2,0,1:T(8,128)(2,1)}), bf16[144,8,768]{2,0,1:T(8,128)(2,1)}, u32[]{:S(2)}, u32[]{:S(2)}) async-start(bf16[144,8,768]{2,0,1:T(8,128)(2,1)} %copy.24), calls=%async_computation | async-start | bytes 3538944 | tf_op jit(solution)/shard_map/all_to_all | solution.py:113
  83.0 13.1 %all_gather.6 = f32[3,32,128]{2,1,0:T(8,128)S(1)} all-gather(f32[3,8,128]{2,1,0:T(8,128)S(1)} %copy-done.6), channel_id=1, replica_groups=mesh['comp'=8,'band'=4] {'band'}, dimensions={1}, use_global_device_ids=true | all-gather | bytes 61440 | tf_op jit(solution)/shard_map/all_gather | solution.py:136
  96.1 1.3 collective-permute-start.8
  97.4 1.5 collective-permute-start.9
  99.1 7.0 %all-to-all-done = bf16[144,8,768]{2,0,1:T(8,128)(2,1)} async-done(((bf16[144,8,768]{2,0,1:T(8,128)(2,1)}), bf16[144,8,768]{2,0,1:T(8,128)(2,1)}, u32[]{:S(2)}, u32[]{:S(2)}) %all-to-all-start) | async-done | bytes 1769504 | tf_op jit(solution)/shard_map/all_to_all | solution.py:113
  106.1 3.9 %copy.25 = bf16[1152,768]{0,1:T(8,128)(2,1)} copy(bf16[1152,768]{1,0:T(8,128)(2,1)} %bitcast.2) | data formatting | bytes 3538944 | tf_op jit(solution)/shard_map/squeeze | solution.py:113
  110.0 1.8 convert_reduce_fusion
  111.8 5.4 %fusion.240 = (f32[768]{0:T(1024)S(1)}, f32[1152,768]{0,1:T(8,128)S(1)}) fusion(f32[768]{0:T(1024)S(1)} %broadcast_multiply_fusion.3, f32[1152]{0:T(1024)S(1)} %copy-done.7, bf16[1152,768]{1,0:T(8,128)(2,1)} %bitcast.2, bf16[1152,1152]{1,0:T(8,128)(2,1)S(1)} %copy-done, bf16[1152,768]{0,1:T(8,128)(2,1)} %copy.25), kind=kOutput, calls=%fused_computation.385 | convolution fusion | flops 2044624128 | bytes 9742848 | tf_op jit(solution)/shard_map/dot_general | solution.py:81
  117.2 3.0 %fusion.241 = (f32[768]{0:T(1024)S(1)}, f32[1152,768]{0,1:T(8,128)S(1)}) fusion(f32[1152,768]{0,1:T(8,128)S(1)} %get-tuple-element.42, f32[768]{0:T(1024)S(1)} %broadcast_multiply_fusion.2, f32[1152]{0:T(1024)S(1)} %copy-done.7, bf16[1152,1152]{1,0:T(8,128)(2,1)S(1)} %copy-done), kind=kOutput, calls=%fused_computation.386 | convolution fusion | flops 2044624128 | bytes 9742848 | tf_op jit(solution)/shard_map/dot_general | solution.py:81
  120.2 2.9 %fusion.242 = (f32[768]{0:T(1024)S(1)}, f32[1152,768]{0,1:T(8,128)S(1)}) fusion(f32[1152,768]{0,1:T(8,128)S(1)} %get-tuple-element.44, f32[768]{0:T(1024)S(1)} %broadcast_multiply_fusion.1, f32[1152]{0:T(1024)S(1)} %copy-done.7, bf16[1152,1152]{1,0:T(8,128)(2,1)S(1)} %copy-done), kind=kOutput, calls=%fused_computation.387 | convolution fusion | flops 2044624128 | bytes 9742848 | tf_op jit(solution)/shard_map/dot_general | solution.py:81
  123.2 4.1 %fusion.66 = bf16[1152,1,768]{0,2,1:T(8,128)(2,1)} fusion(bf16[1152,768]{0,1:T(8,128)(2,1)S(1)} %copy-done.4, f32[1152,768]{0,1:T(8,128)S(1)} %get-tuple-element.46, bf16[1152,1152]{1,0:T(8,128)(2,1)S(1)} %copy-done, f32[768]{0:T(1024)S(1)} %broadcast_multiply_fusion, f32[1152]{0:T(1024)S(1)} %copy-done.7), kind=kOutput, calls=%fused_computation.93 | convolution fusion | flops 2046394368 | bytes 9739776 | tf_op jit(solution)/shard_map/dot_general | solution.py:81
  127.3 0.5 broadcast.883
  127.8 3.5 %reduce.1 = bf16[1152,768]{0,1:T(8,128)(2,1)S(1)} reduce(bf16[1152,1,768]{0,2,1:T(8,128)(2,1)} %fusion.66, bf16[]{:T(256)} %broadcast.883), dimensions={1}, to_apply=%copy.26.reduce_sub_computation | reduce | bytes 3538946 | tf_op jit(solution)/shard_map/broadcast_in_dim | solution.py:119
  131.2 2.3 copy.35
  133.5 5.8 %reshape.300 = bf16[8,2,55296]{2,1,0:T(2,128)(2,1)} reshape(bf16[1152,768]{1,0:T(8,128)(2,1)} %copy.35) | data formatting | bytes 3538944
  139.3 4.5 %all-to-all-start.1 = ((bf16[8,2,55296]{2,1,0:T(2,128)(2,1)}), bf16[8,2,55296]{2,1,0:T(2,128)(2,1)}, u32[]{:S(2)}, u32[]{:S(2)}) async-start(bf16[8,2,55296]{2,1,0:T(2,128)(2,1)} %reshape.300), calls=%async_computation.1 | async-start | bytes 3538944 | tf_op jit(solution)/shard_map/all_to_all | solution.py:118
  144.2 2.1 copy.32
  146.2 20.5 %all-to-all-done.1 = bf16[8,2,55296]{2,1,0:T(2,128)(2,1)} async-done(((bf16[8,2,55296]{2,1,0:T(2,128)(2,1)}), bf16[8,2,55296]{2,1,0:T(2,128)(2,1)}, u32[]{:S(2)}, u32[]{:S(2)}) %all-to-all-start.1) | async-done | bytes 1769504 | tf_op jit(solution)/shard_map/all_to_all | solution.py:118
  166.8 6.6 %reshape.301 = bf16[1152,1,768]{2,1,0:T(2,128)(2,1)} reshape(bf16[8,2,55296]{2,1,0:T(2,128)(2,1)} %all-to-all-done.1) | data formatting | bytes 3538944
  173.3 2.3 copy.27
  175.6 0.3 fusion.243
  175.9 0.4 copy.33
  176.3 1.6 copy-done.3
  177.9 1.9 fusion
  179.8 22.8 %psum.7 = bf16[3,6144]{1,0:T(4,128)(2,1)S(1)} all-reduce(bf16[3,6144]{1,0:T(4,128)(2,1)S(1)} %fusion), channel_id=1, replica_groups=mesh['comp'=8,'band'=4] {'comp'}, use_global_device_ids=true, to_apply=%region_4.5 | all-reduce | flops 18432 | bytes 73728 | tf_op jit(solution)/shard_map/psum | solution.py:126
  202.6 2.0 copy.30
  204.6 12.7 %gather_fusion = f32[3072,3]{1,0:T(8,128)} fusion(f32[3,6144]{0,1:T(8,128)} %copy.30, s32[3072]{0:T(1024)S(1)} %broadcast_clamp_fusion), kind=kCustom, calls=%fused_computation | custom fusion | bytes 86016 | tf_op jit(solution)/shard_map/jit(_take)/gather | solution.py:130
  217.3 1.9 copy.31
  219.2 13.1 %all-gather = f32[3,1,32,128]{3,2,0,1:T(8,128)S(1)} all-gather(f32[3,1,8,128]{3,2,0,1:T(8,128)S(1)} %fusion.213), channel_id=2, replica_groups=mesh['comp'=8,'band'=4] {'band'}, dimensions={2}, use_global_device_ids=true | all-gather | bytes 61440 | tf_op jit(solution)/shard_map/all_gather | solution.py:137
  232.4 1.3 collective-permute-start.10
  233.6 1.3 collective-permute-start.11
  234.9 0.3 convert_bitcast_fusion
  235.3 3.8 %copy.28 = f32[144,8,1,768]{3,1,0,2:T(8,128)} copy(f32[144,8,1,768]{3,0,1,2:T(8,128)S(1)} %convert_bitcast_fusion) | data formatting | bytes 7077888 | tf_op jit(solution)/shard_map/convert_element_type | solution.py:121
  239.1 4.8 %reshape.286 = f32[144,24,256]{2,1,0:T(8,128)} reshape(f32[144,8,1,768]{3,1,0,2:T(8,128)} %copy.28) | data formatting | bytes 7077888 | tf_op jit(solution)/shard_map/convert_element_type | solution.py:121
  243.9 5.5 %add.481 = f32[144,24,256]{2,1,0:T(8,128)} add(f32[144,24,256]{2,1,0:T(8,128)} %get-tuple-element.7, f32[144,24,256]{2,1,0:T(8,128)} %reshape.286) | non-fusion elementwise | flops 884736 | bytes 10616832 | tf_op jit(solution)/shard_map/add | solution.py:127
  249.4 0.2 select_maximum_fusion
  251.0 0.7 fusion.212
  (54 shorter events, 2.1 us)
Async XLA Ops:
  0.6 111.1 %copy-start = (bf16[1152,1152]{1,0:T(8,128)(2,1)S(1)}, bf16[1152,1152]{1,0:T(8,128)(2,1)}, u32[]{:S(2)}) copy-start(bf16[1152,1152]{1,0:T(8,128)(2,1)} %param.8) | copy-start | bytes 7962628
  2.6 8.0 %collective-permute-start = (f32[144,1,256]{2,1,0:T(1,128)S(1)}, f32[144,1,256]{2,1,0:T(1,128)S(1)}, u32[]{:S(2)}, u32[]{:S(2)}) collective-permute-start(f32[144,1,256]{2,1,0:T(1,128)S(1)} %get-tuple-element.14), channel_id=1, source_target_pairs={{0,1},{1,2},{2,3},{4,5},{5,6},{6,7},{8,9},{9,10},{10,11},{12,13},{... | collective-permute-start | bytes 442376 | tf_op jit(solution)/shard_map/ppermute | solution.py:29
  7.6 7.2 %collective-permute-start.1 = (f32[144,1,256]{2,1,0:T(1,128)S(1)}, f32[144,1,256]{2,1,0:T(1,128)S(1)}, u32[]{:S(2)}, u32[]{:S(2)}) collective-permute-start(f32[144,1,256]{2,1,0:T(1,128)S(1)} %get-tuple-element.15), channel_id=1, source_target_pairs={{1,0},{2,1},{3,2},{5,4},{6,5},{7,6},{9,8},{10,9},{11,10},{13,12},{... | collective-permute-start | bytes 442376 | tf_op jit(solution)/shard_map/ppermute | solution.py:31
  26.0 6.1 %collective-permute-start.2 = (f32[144,1,256]{2,1,0:T(1,128)S(1)}, f32[144,1,256]{2,1,0:T(1,128)S(1)}, u32[]{:S(2)}, u32[]{:S(2)}) collective-permute-start(f32[144,1,256]{2,1,0:T(1,128)S(1)} %get-tuple-element.12), channel_id=1, source_target_pairs={{0,1},{1,2},{2,3},{4,5},{5,6},{6,7},{8,9},{9,10},{10,11},{12,13},{... | collective-permute-start | bytes 442376 | tf_op jit(solution)/shard_map/ppermute | solution.py:29
  29.5 7.0 %collective-permute-start.3 = (f32[144,1,256]{2,1,0:T(1,128)S(1)}, f32[144,1,256]{2,1,0:T(1,128)S(1)}, u32[]{:S(2)}, u32[]{:S(2)}) collective-permute-start(f32[144,1,256]{2,1,0:T(1,128)S(1)} %get-tuple-element.13), channel_id=1, source_target_pairs={{1,0},{2,1},{3,2},{5,4},{6,5},{7,6},{9,8},{10,9},{11,10},{13,12},{... | collective-permute-start | bytes 442376 | tf_op jit(solution)/shard_map/ppermute | solution.py:31
  41.4 6.1 %collective-permute-start.4 = (f32[144,1,256]{2,1,0:T(1,128)S(1)}, f32[144,1,256]{2,1,0:T(1,128)S(1)}, u32[]{:S(2)}, u32[]{:S(2)}) collective-permute-start(f32[144,1,256]{2,1,0:T(1,128)S(1)} %get-tuple-element.10), channel_id=1, source_target_pairs={{0,1},{1,2},{2,3},{4,5},{5,6},{6,7},{8,9},{9,10},{10,11},{12,13},{... | collective-permute-start | bytes 442376 | tf_op jit(solution)/shard_map/ppermute | solution.py:29
  44.9 7.0 %collective-permute-start.5 = (f32[144,1,256]{2,1,0:T(1,128)S(1)}, f32[144,1,256]{2,1,0:T(1,128)S(1)}, u32[]{:S(2)}, u32[]{:S(2)}) collective-permute-start(f32[144,1,256]{2,1,0:T(1,128)S(1)} %get-tuple-element.11), channel_id=1, source_target_pairs={{1,0},{2,1},{3,2},{5,4},{6,5},{7,6},{9,8},{10,9},{11,10},{13,12},{... | collective-permute-start | bytes 442376 | tf_op jit(solution)/shard_map/ppermute | solution.py:31
  56.8 4.6 %collective-permute-start.6 = (f32[144,1,256]{2,1,0:T(1,128)S(1)}, f32[144,1,256]{2,1,0:T(1,128)S(1)}, u32[]{:S(2)}, u32[]{:S(2)}) collective-permute-start(f32[144,1,256]{2,1,0:T(1,128)S(1)} %get-tuple-element.8), channel_id=1, source_target_pairs={{0,1},{1,2},{2,3},{4,5},{5,6},{6,7},{8,9},{9,10},{10,11},{12,13},{... | collective-permute-start | bytes 442376 | tf_op jit(solution)/shard_map/ppermute | solution.py:29
  58.7 7.0 %collective-permute-start.7 = (f32[144,1,256]{2,1,0:T(1,128)S(1)}, f32[144,1,256]{2,1,0:T(1,128)S(1)}, u32[]{:S(2)}, u32[]{:S(2)}) collective-permute-start(f32[144,1,256]{2,1,0:T(1,128)S(1)} %get-tuple-element.9), channel_id=1, source_target_pairs={{1,0},{2,1},{3,2},{5,4},{6,5},{7,6},{9,8},{10,9},{11,10},{13,12},{... | collective-permute-start | bytes 442376 | tf_op jit(solution)/shard_map/ppermute | solution.py:31
  75.6 7.4 %copy-start.6 = (f32[3,8,128]{2,1,0:T(8,128)S(1)}, f32[3,8,128]{2,1,0:T(8,128)}, u32[]{:S(2)}) copy-start(f32[3,8,128]{2,1,0:T(8,128)} %param.10) | copy-start | bytes 36868
  75.6 23.5 %copy-start.5 = (s32[3,8,128]{2,1,0:T(8,128)S(1)}, s32[3,8,128]{2,1,0:T(8,128)}, u32[]{:S(2)}) copy-start(s32[3,8,128]{2,1,0:T(8,128)} %param.11) | copy-start | bytes 36868
  78.6 27.5 %all-to-all-start = ((bf16[144,8,768]{2,0,1:T(8,128)(2,1)}), bf16[144,8,768]{2,0,1:T(8,128)(2,1)}, u32[]{:S(2)}, u32[]{:S(2)}) async-start(bf16[144,8,768]{2,0,1:T(8,128)(2,1)} %copy.24), calls=%async_computation | async-start | bytes 3538944 | tf_op jit(solution)/shard_map/all_to_all | solution.py:113
  83.0 28.8 %copy-start.7 = (f32[1152]{0:T(1024)S(1)}, f32[1152]{0:T(1024)}, u32[]{:S(2)}) copy-start(f32[1152]{0:T(1024)} %param.9) | copy-start | bytes 13828
  96.1 47.8 %collective-permute-start.8 = (f32[3,32,17]{2,1,0:T(8,128)S(1)}, f32[3,32,17]{2,1,0:T(8,128)S(1)}, u32[]{:S(2)}, u32[]{:S(2)}) collective-permute-start(f32[3,32,17]{2,1,0:T(8,128)S(1)} %get-tuple-element.25), channel_id=1, source_target_pairs={{0,4},{4,8},{8,12},{12,16},{16,20},{20,24},{24,28},{1,5},{5,9},{9,... | collective-permute-start | bytes 19592 | tf_op jit(solution)/shard_map/ppermute | solution.py:29
  97.4 46.5 %collective-permute-start.9 = (f32[3,32,17]{2,1,0:T(8,128)S(1)}, f32[3,32,17]{2,1,0:T(8,128)S(1)}, u32[]{:S(2)}, u32[]{:S(2)}) collective-permute-start(f32[3,32,17]{2,1,0:T(8,128)S(1)} %get-tuple-element.26), channel_id=1, source_target_pairs={{4,0},{8,4},{12,8},{16,12},{20,16},{24,20},{28,24},{5,1},{9,5},{13... | collective-permute-start | bytes 19592 | tf_op jit(solution)/shard_map/ppermute | solution.py:31
  120.2 3.0 %copy-start.4 = (bf16[1152,768]{0,1:T(8,128)(2,1)S(1)}, bf16[1152,768]{0,1:T(8,128)(2,1)}, u32[]{:S(2)}) copy-start(bf16[1152,768]{0,1:T(8,128)(2,1)} %copy.25) | copy-start | bytes 5308420
  133.5 10.6 %copy-start.2 = (bf16[144,24,256]{2,1,0:T(8,128)(2,1)S(1)}, bf16[144,24,256]{2,1,0:T(8,128)(2,1)}, u32[]{:S(2)}) copy-start(bf16[144,24,256]{2,1,0:T(8,128)(2,1)} %get-tuple-element.6) | copy-start | bytes 5308420
  139.3 27.5 %all-to-all-start.1 = ((bf16[8,2,55296]{2,1,0:T(2,128)(2,1)}), bf16[8,2,55296]{2,1,0:T(2,128)(2,1)}, u32[]{:S(2)}, u32[]{:S(2)}) async-start(bf16[8,2,55296]{2,1,0:T(2,128)(2,1)} %reshape.300), calls=%async_computation.1 | async-start | bytes 3538944 | tf_op jit(solution)/shard_map/all_to_all | solution.py:118
  175.9 2.0 copy-start.3
  232.4 17.0 %collective-permute-start.10 = (f32[3,32,17]{2,1,0:T(8,128)S(1)}, f32[3,32,17]{2,1,0:T(8,128)S(1)}, u32[]{:S(2)}, u32[]{:S(2)}) collective-permute-start(f32[3,32,17]{2,1,0:T(8,128)S(1)} %get-tuple-element.23), channel_id=1, source_target_pairs={{0,4},{4,8},{8,12},{12,16},{16,20},{20,24},{24,28},{1,5},{5,9},{9,... | collective-permute-start | bytes 19592 | tf_op jit(solution)/shard_map/ppermute | solution.py:29
  233.6 15.7 %collective-permute-start.11 = (f32[3,32,17]{2,1,0:T(8,128)S(1)}, f32[3,32,17]{2,1,0:T(8,128)S(1)}, u32[]{:S(2)}, u32[]{:S(2)}) collective-permute-start(f32[3,32,17]{2,1,0:T(8,128)S(1)} %get-tuple-element.24), channel_id=1, source_target_pairs={{4,0},{8,4},{12,8},{16,12},{20,16},{24,20},{28,24},{5,1},{9,5},{13... | collective-permute-start | bytes 19592 | tf_op jit(solution)/shard_map/ppermute | solution.py:31
  243.9 7.8 %copy-start.1 = (bf16[1152,1152]{1,0:T(8,128)(2,1)S(1)}, bf16[1152,1152]{1,0:T(8,128)(2,1)}, u32[]{:S(2)}) copy-start(bf16[1152,1152]{1,0:T(8,128)(2,1)} %param.8) | copy-start | bytes 7962628
where the time goes:
time: 255 us; the launch traced here: 252 us
  local copies, waits for them, and re-layouts  60.3 us (24%)
  waiting for transfers between devices  49.8 us (20%)
  blocking collectives  48.9 us (19%)
  other arithmetic  41.1 us (16%)
  starting transfers between devices  33.2 us (13%)
  matrix products  17.3 us (7%)
    psum x1, blocking collectives, on_device(): lax.psum(partial_value.astype(jnp.bfloat16), 'comp').astype(jnp.float32)  22.8 us
    all_to_all x1, waiting for transfers between devices, on_device(): lax.all_to_all(increment[:, None, :], 'comp', split_axis=0, concat_axis=1...  20.5 us
    mul x3, other arithmetic, upwind(): return (middle - flux_rows - flux_cols) * wet_rows  20.3 us
    unnamed x21, local copies, waits for them, and re-layouts  18.7 us
    ppermute x6, waiting for transfers between devices, extended_2(): lax.ppermute(head, axis, [((i + 1) % count, i) for i in range(ends)])  17.3 us
    ppermute x6, starting transfers between devices, extended_2(): lax.ppermute(tail, axis, [(i, (i + 1) % count) for i in range(ends)])  16.4 us
    dot_general x4, matrix products, sources(): jnp.dot(quad_matrix, current.astype(jnp.bfloat16), preferred_element_type...  15.4 us
    gather x2, local copies, waits for them, and re-layouts, on_device(): jnp.take(band_stress, source_points.reshape(-1), axis=1)  14.6 us
  transfers between devices with their start and end apart: 14, of which 10 were waited for; matrix products, arithmetic and copies ran while one was open for 20% of the time, Pallas kernels for 0%

commit v1 on v0

v1 whole, which is shorter than its diff:
```python
import functools
import math

import jax
import jax.numpy as jnp
from jax import lax
from jax.experimental import pallas as pl
from jax.experimental.pallas import tpu as pltpu
from jax.sharding import PartitionSpec as P

NF = 36
ND = 32
SUBSTEPS = 4
SRC_STEPS = 4
SW_STEPS = 8
COMP_BLOCK = 16
LANES = 128
VMEM_LIMIT = 50 * 1024 * 1024

step_source = 0.1
wave_speed = 0.35
friction = 0.05
forcing_gain = 0.15


def neighbours(cells, axis, dim, width):
    count = lax.axis_size(axis)
    ends = count - 1
    head = lax.slice_in_dim(cells, 0, width, axis=dim)
    tail = lax.slice_in_dim(cells, cells.shape[dim] - width, cells.shape[dim], axis=dim)
    before = lax.ppermute(tail, axis, [(i, i + 1) for i in range(ends)])
    after = lax.ppermute(head, axis, [(i + 1, i) for i in range(ends)])
    return before, after


def component_tables(offset, local_count, freqs, headings):
    indices = offset + jnp.arange(local_count, dtype=jnp.int32)
    frequency = (indices // headings).astype(jnp.float32)
    heading = (indices % headings).astype(jnp.float32)
    heading_angle = 2.0 * math.pi * (heading + 0.5) / headings
    fraction = (frequency + 0.5) / freqs
    group_speed = 0.25 + 0.4 * fraction
    wave_ratio = 0.5 + 0.5 * fraction
    cosine = jnp.cos(heading_angle)
    sine_part = jnp.sin(heading_angle)
    stress_coef = jnp.stack(
        [
            wave_ratio * (1.0 + cosine * cosine) - 0.5,
            wave_ratio * sine_part * cosine,
            wave_ratio * (1.0 + sine_part * sine_part) - 0.5,
        ]
    )
    return (group_speed * cosine, group_speed * sine_part, stress_coef)


def propagate_kernel(rows, *refs):
    x_refs = refs[:-6]
    before_ref, after_ref, wet_ref, speed_ref, dens_ref, sent_ref = refs[-6:]
    columns = dens_ref.shape[2]
    lane = lax.broadcasted_iota(jnp.int32, (8, columns), 1)
    before = before_ref[...].astype(jnp.float32)
    after = after_ref[...].astype(jnp.float32)
    total = rows + 2 * SUBSTEPS
    for half in range(COMP_BLOCK // 8):
        c0 = half * 8
        ax = jnp.broadcast_to(speed_ref[c0 : c0 + 8, 0:1], (8, columns))
        ay = jnp.broadcast_to(speed_ref[c0 : c0 + 8, 1:2], (8, columns))
        keep = 1.0 - jnp.abs(ax) - jnp.abs(ay)
        west, east = jnp.maximum(ax, 0.0), jnp.maximum(-ax, 0.0)
        south = jnp.where(lane > 0, jnp.maximum(ay, 0.0), 0.0)
        north = jnp.where(lane < columns - 1, jnp.maximum(-ay, 0.0), 0.0)
        stages = [dict() for _ in range(SUBSTEPS + 1)]
        for r in range(total):
            if r < SUBSTEPS:
                stages[0][r] = before[r, c0 : c0 + 8]
            elif r < SUBSTEPS + rows:
                part = pl.ds(c0 * rows + r - SUBSTEPS, 8, stride=rows)
                stages[0][r] = jnp.concatenate([x_ref[part, :] for x_ref in x_refs], axis=1)
            else:
                stages[0][r] = after[r - SUBSTEPS - rows, c0 : c0 + 8]
            for s in range(1, SUBSTEPS + 1):
                q = r - s
                if q < s or q >= total - s:
                    continue
                old = stages[s - 1]
                middle = old[q]
                value = (
                    keep * middle
                    + west * old[q - 1]
                    + east * old[q + 1]
                    + south * pltpu.roll(middle, 1, 1)
                    + north * pltpu.roll(middle, columns - 1, 1)
                ) * wet_ref[q : q + 1, :]
                stages[s][q] = value
                if s == SUBSTEPS:
                    dens_ref[q - SUBSTEPS, c0 : c0 + 8, :] = value
    sent_ref[...] = dens_ref[...].astype(jnp.bfloat16)


def propagate(spectrum, before, after, wet, speeds):
    count, rows, columns = spectrum.shape
    grid = (pl.cdiv(count, COMP_BLOCK),)
    parts = columns // LANES
    flat = spectrum.reshape(count * rows, columns)
    return pl.pallas_call(
        functools.partial(propagate_kernel, rows),
        grid=grid,
        in_specs=[
            pl.BlockSpec((COMP_BLOCK * rows, LANES), functools.partial(lambda p, i: (i, p), p))
            for p in range(parts)
        ]
        + [
            pl.BlockSpec((SUBSTEPS, COMP_BLOCK, columns), lambda i: (0, i, 0)),
            pl.BlockSpec((SUBSTEPS, COMP_BLOCK, columns), lambda i: (0, i, 0)),
            pl.BlockSpec((rows + 2 * SUBSTEPS, columns), lambda i: (0, 0)),
            pl.BlockSpec((COMP_BLOCK, 2), lambda i: (i, 0)),
        ],
        out_specs=[
            pl.BlockSpec((rows, COMP_BLOCK, columns), lambda i: (0, i, 0)),
            pl.BlockSpec((rows, COMP_BLOCK, columns), lambda i: (0, i, 0)),
        ],
        out_shape=[
            jax.ShapeDtypeStruct((rows, count, columns), jnp.float32),
            jax.ShapeDtypeStruct((rows, count, columns), jnp.bfloat16),
        ],
        compiler_params=pltpu.CompilerParams(vmem_limit_bytes=VMEM_LIMIT),
    )(*[flat] * parts, before, after, wet, speeds)


def finish_kernel(rows, dens_ref, inc_ref, out_ref, *parts):
    for r in range(rows):
        value = dens_ref[r] + inc_ref[r].astype(jnp.float32)
        for c0 in range(0, COMP_BLOCK, 8):
            for p, part in enumerate(parts):
                part[pl.ds(c0 * rows + r, 8, stride=rows), :] = value[
                    c0 : c0 + 8, p * LANES : (p + 1) * LANES
                ]
    for p, part in enumerate(parts):
        out_ref[:, p * LANES : (p + 1) * LANES] = part[...]


def finish(density, increment):
    rows, count, columns = density.shape
    spec = pl.BlockSpec((rows, COMP_BLOCK, columns), lambda i: (0, i, 0))
    out = pl.pallas_call(
        functools.partial(finish_kernel, rows),
        grid=(pl.cdiv(count, COMP_BLOCK),),
        in_specs=[spec, spec],
        out_specs=pl.BlockSpec((COMP_BLOCK * rows, columns), lambda i: (i, 0)),
        out_shape=jax.ShapeDtypeStruct((count * rows, columns), jnp.float32),
        scratch_shapes=[pltpu.VMEM((COMP_BLOCK * rows, LANES), jnp.float32)] * (columns // LANES),
        compiler_params=pltpu.CompilerParams(vmem_limit_bytes=VMEM_LIMIT),
    )(density, increment)
    return out.reshape(count, rows, columns)


def row_sources(base_ref, quad_ref, diss_ref, coef_ref, cur, low, inc_ref):
    blocks, count, columns = base_ref.shape
    total = blocks * count
    tiles = 3
    tile = total // tiles
    base = base_ref[...].reshape(total, columns)
    low[0] = base
    cur[...] = base.astype(jnp.float32)
    level = jnp.sum(cur[...], axis=0, keepdims=True)
    for s in range(SRC_STEPS):
        after = jnp.zeros_like(level)
        for t in range(tiles):
            part = slice(t * tile, (t + 1) * tile)
            product = jnp.dot(quad_ref[part, :], low[s % 2], preferred_element_type=jnp.float32)
            now = cur[part, :]
            now = now + step_source * now * (product - diss_ref[part, :] * (level / total))
            cur[part, :] = now
            after = after + jnp.sum(now, axis=0, keepdims=True)
            if s < SRC_STEPS - 1:
                low[(s + 1) % 2, part, :] = now.astype(jnp.bfloat16)
        level = after
    wide = base_ref[...].reshape(total, columns).astype(jnp.float32)
    increment = (cur[...] - wide).astype(jnp.bfloat16)
    inc_ref[...] = increment.reshape(blocks, count, columns)
    coupled = wide + increment.astype(jnp.float32)
    return (
        jnp.dot(
            coef_ref[...],
            coupled,
            precision=lax.Precision.HIGHEST,
            preferred_element_type=jnp.float32,
        )
        / total
    )


def sources_kernel(base_ref, quad_ref, diss_ref, coef_ref, inc_ref, stress_ref, cur, low):
    stress_ref[0] = row_sources(
        base_ref.at[:, 0], quad_ref, diss_ref, coef_ref, cur, low, inc_ref.at[:, 0]
    )


def sources(base, quad_matrix, dissipation, coef):
    blocks, rows, count, columns = base.shape
    total = blocks * count
    return pl.pallas_call(
        sources_kernel,
        grid=(rows,),
        in_specs=[
            pl.BlockSpec((blocks, 1, count, columns), lambda i: (0, i, 0, 0)),
            pl.BlockSpec((total, total), lambda i: (0, 0)),
            pl.BlockSpec((total, 1), lambda i: (0, 0)),
            pl.BlockSpec(coef.shape, lambda i: (0, 0)),
        ],
        out_specs=[
            pl.BlockSpec((blocks, 1, count, columns), lambda i: (0, i, 0, 0)),
            pl.BlockSpec((1, coef.shape[0], columns), lambda i: (i, 0, 0)),
        ],
        out_shape=[
            jax.ShapeDtypeStruct(base.shape, jnp.bfloat16),
            jax.ShapeDtypeStruct((rows, coef.shape[0], columns), jnp.float32),
        ],
        scratch_shapes=[
            pltpu.VMEM((total, columns), jnp.float32),
            pltpu.VMEM((2, total, columns), jnp.bfloat16),
        ],
        compiler_params=pltpu.CompilerParams(vmem_limit_bytes=VMEM_LIMIT),
    )(base, quad_matrix, dissipation, coef)


def pick_kernel(table_ref, index_ref, out_ref):
    high = table_ref.shape[2]
    cells = index_ref.shape[2]
    table = table_ref[0].reshape(3 * high, LANES)
    result = [jnp.zeros((1, cells), jnp.float32) for _ in range(3)]
    for m, weight in enumerate((0.5, 0.3, 0.2)):
        index = index_ref[0, m : m + 1, :]
        low = index % LANES
        top = index // LANES
        lane_hit = lax.broadcasted_iota(jnp.int32, (LANES, cells), 0) == low
        ones = jnp.where(lane_hit, 1.0, 0.0).astype(jnp.bfloat16)
        spread = jnp.dot(table, ones, preferred_element_type=jnp.float32)
        row_hit = lax.broadcasted_iota(jnp.int32, (high, cells), 0) == top
        for k in range(3):
            part = jnp.where(row_hit, spread[k * high : (k + 1) * high], 0.0)
            result[k] = result[k] + weight * jnp.sum(part, axis=0, keepdims=True)
    out_ref[0] = jnp.concatenate(result, axis=0)


def pick(table, index):
    bands, _, high, _ = table.shape
    cells = index.shape[2]
    return pl.pallas_call(
        pick_kernel,
        grid=(bands,),
        in_specs=[
            pl.BlockSpec((1, 3, high, LANES), lambda b: (b, 0, 0, 0)),
            pl.BlockSpec((1, 3, cells), lambda b: (b, 0, 0)),
        ],
        out_specs=pl.BlockSpec((1, 3, cells), lambda b: (b, 0, 0)),
        out_shape=jax.ShapeDtypeStruct((bands, 3, cells), jnp.float32),
        compiler_params=pltpu.CompilerParams(vmem_limit_bytes=VMEM_LIMIT),
    )(table, index)


def diff_rows(extended):
    return 0.5 * (extended[2:, 1:-1] - extended[:-2, 1:-1])


def diff_cols(extended):
    return 0.5 * (extended[1:-1, 2:] - extended[1:-1, :-2])


def exchange_sources(sent, quad_matrix, dissipation, coef, groups):
    rows, count, columns = sent.shape
    own = rows // groups
    arrived = lax.all_to_all(sent, "comp", split_axis=0, concat_axis=0, tiled=True)
    base = arrived.reshape(groups, own, count, columns)
    if count % 16:
        base = base.transpose(1, 0, 2, 3).reshape(1, own, groups * count, columns)
    increment, stress = sources(base, quad_matrix, dissipation[:, None], coef)
    if count % 16:
        increment = increment.reshape(own, groups, count, columns).transpose(1, 0, 2, 3)
    returned = lax.all_to_all(
        increment.reshape(rows, count, columns), "comp", split_axis=0, concat_axis=0, tiled=True
    )
    return returned, stress


def on_device(spectrum, wet_mask, quad_matrix, dissipation, circulation, source_points):
    local_count, row_count, columns = spectrum.shape
    groups = lax.axis_size("comp")
    bands = lax.axis_size("band")
    own_rows = row_count // groups
    offset = lax.axis_index("comp") * local_count
    speed_x, speed_y, _ = component_tables(offset, local_count, NF, ND)
    stress_coef = component_tables(0, local_count * groups, NF, ND)[2]
    coef = jnp.pad(stress_coef, ((0, 5), (0, 0)))

    head = spectrum[:, :SUBSTEPS].transpose(1, 0, 2).astype(jnp.bfloat16)
    tail = spectrum[:, row_count - SUBSTEPS :].transpose(1, 0, 2).astype(jnp.bfloat16)
    before, after = neighbours(jnp.concatenate([head, tail], axis=0), "band", 0, SUBSTEPS)
    wet = wet_mask.astype(jnp.float32)
    wet_before, wet_after = neighbours(wet, "band", 0, SUBSTEPS)
    wet = jnp.concatenate([wet_before, wet, wet_after], axis=0)
    density, sent = propagate(
        spectrum, before, after, wet, jnp.stack([speed_x, speed_y], axis=1)
    )

    tile_rows = circulation.shape[1]
    tile_cols = circulation.shape[2]
    margin = 2 * SW_STEPS + 1
    both = jnp.concatenate([circulation, source_points.astype(jnp.float32)], axis=0)
    both = lax.all_gather(both, "band", axis=1, tiled=True)
    left, right = neighbours(both, "comp", 2, margin)
    wide = jnp.concatenate([left, both, right], axis=2)
    wide_cols = wide.shape[2]
    padded_cols = pl.cdiv(wide_cols, LANES) * LANES
    index = jnp.pad(wide[3:].astype(jnp.int32), ((0, 0), (0, 0), (0, padded_cols - wide_cols)))
    index = index.reshape(3, bands, tile_rows * padded_cols).transpose(1, 0, 2)

    increment, stress = exchange_sources(sent, quad_matrix, dissipation, coef, groups)
    own_stress = stress[:, :3].transpose(1, 0, 2).reshape(3, -1).astype(jnp.bfloat16)
    table = lax.all_gather(own_stress, ("band", "comp"), axis=0)
    table = table.reshape(bands, groups, 3, own_rows * columns // LANES, LANES)
    table = table.transpose(0, 2, 1, 3, 4).reshape(bands, 3, -1, LANES)
    cell_stress = pick(table, index).reshape(bands, 3, tile_rows, padded_cols)
    cell_stress = cell_stress.transpose(1, 0, 2, 3).reshape(3, -1, padded_cols)[..., :wide_cols]
    new_spectrum = finish(density, increment)

    global_col = (
        lax.axis_index("comp") * tile_cols - margin + jnp.arange(wide_cols, dtype=jnp.int32)
    )
    inside = ((global_col >= 0) & (global_col < tile_cols * groups)).astype(jnp.float32)[None, :]
    rimmed = jnp.pad(cell_stress * inside, ((0, 0), (1, 1), (1, 1)))
    force_down = -(diff_rows(rimmed[0]) + diff_cols(rimmed[1]))
    force_across = -(diff_rows(rimmed[1]) + diff_cols(rimmed[2]))
    height, flow_down, flow_across = wide[0], wide[1], wide[2]
    for repeat in range(SW_STEPS):
        down_ext = jnp.pad(flow_down, 1)
        across_ext = jnp.pad(flow_across, 1)
        height = (height - wave_speed * (diff_rows(down_ext) + diff_cols(across_ext))) * inside
        height_ext = jnp.pad(height, 1)
        flow_down = (
            (1.0 - friction) * flow_down
            - wave_speed * diff_rows(height_ext)
            + forcing_gain * force_down
        ) * inside
        flow_across = (
            (1.0 - friction) * flow_across
            - wave_speed * diff_cols(height_ext)
            + forcing_gain * force_across
        ) * inside
    stacked = jnp.stack([height, flow_down, flow_across])
    row_start = lax.axis_index("band") * tile_rows
    own = lax.dynamic_slice_in_dim(stacked, row_start, tile_rows, 1)
    return (new_spectrum, own[:, :, margin : margin + tile_cols])


def solution(mesh):
    in_specs = (
        P("comp", "band", None),
        P("band", None),
        P(),
        P(),
        P(None, "band", "comp"),
        P(None, "band", "comp"),
    )
    out_specs = (P("comp", "band", None), P(None, "band", "comp"))
    return jax.shard_map(
        on_device, mesh=mesh, in_specs=in_specs, out_specs=out_specs, check_vma=False
    )
```

time: 255 us -> 175 us (0.69); the launches traced: 252 us -> 175 us
  local copies, waits for them, and re-layouts: 60.3 us -> 5.28 us
  Pallas kernels: 0 us -> 53.4 us
  other arithmetic: 41.1 us -> 3.57 us
  matrix products: 17.3 us -> 0 us
  waiting for transfers between devices: 49.8 us -> 35.7 us
  starting transfers between devices: 33.2 us -> 22.1 us
  blocking collectives: 48.9 us -> 53.4 us
    pallas_call x0 -> x4, Pallas kernels: none -> 53.4 us  [the longest x1 25.7 us: propagate(): pl.pallas_call(functools.partial(propagate_kernel, rows), grid=grid, in_s...]
    all_gather x2, blocking collectives: 26.1 us -> 53.4 us  [the longest x1 39.9 us: on_device(): table = lax.all_gather(own_stress, ('band', 'comp'), axis=0)]
    psum x1 -> x0, blocking collectives: 22.8 us -> none  [on_device(): lax.psum(partial_value.astype(jnp.bfloat16), 'comp').astype(jnp.float32)]
    mul x3 -> x2, other arithmetic: 20.3 us -> 0.08 us  [the longest x1 0.07 us: component_tables(): return (group_speed * cosine, group_speed * sine_part, stress_coef)]
    dot_general x5 -> x0, matrix products: 17.3 us -> none  [the longest x4 15.4 us: sources(): jnp.dot(quad_matrix, current.astype(jnp.bfloat16), preferred_element_type...]
    gather x2 -> x0, local copies, waits for them, and re-layouts: 14.6 us -> none  [on_device(): jnp.take(band_stress, source_points.reshape(-1), axis=1)]
    unnamed x21 -> x9, local copies, waits for them, and re-layouts: 18.7 us -> 4.19 us
    convert_element_type x3 -> x1, local copies, waits for them, and re-layouts: 10.6 us -> 0.04 us  [on_device(): head = spectrum[:, :SUBSTEPS].transpose(1, 0, 2).astype(jnp.bfloat16)]
  transfers between devices with their start and end apart: 14 -> 8, of which waited for: 10 -> 5; matrix products, arithmetic and copies ran while one was open for 20% -> 3% of each run, Pallas kernels for 0% -> 0%
where the time goes in v1:
time: 175 us
  Pallas kernels  53.4 us (31%)
  blocking collectives  53.4 us (31%)
  waiting for transfers between devices  35.7 us (20%)
  starting transfers between devices  22.1 us (13%)
  local copies, waits for them, and re-layouts  5.28 us (3%)
  other arithmetic  3.57 us (2%)
    all_gather x1, blocking collectives, on_device(): table = lax.all_gather(own_stress, ('band', 'comp'), axis=0)  39.9 us
    pallas_call x1, Pallas kernels, propagate(): pl.pallas_call(functools.partial(propagate_kernel, rows), grid=grid, in_s...  25.7 us
    all_to_all x1, waiting for transfers between devices, exchange_sources(): lax.all_to_all(increment.reshape(rows, count, columns), 'comp', split_axi...  21.6 us
    pallas_call x1, Pallas kernels, sources(): pl.pallas_call(sources_kernel, grid=(rows,), in_specs=[pl.BlockSpec((bloc...  16.5 us
    all_gather x1, blocking collectives, on_device(): both = lax.all_gather(both, 'band', axis=1, tiled=True)  13.5 us
    ppermute x3, starting transfers between devices, neighbours(): before = lax.ppermute(tail, axis, [(i, i + 1) for i in range(ends)])  10.8 us
    ppermute x3, waiting for transfers between devices, neighbours(): after = lax.ppermute(head, axis, [(i + 1, i) for i in range(ends)])  7.64 us
    pallas_call x1, Pallas kernels, finish(): pl.pallas_call(functools.partial(finish_kernel, rows), grid=(pl.cdiv(coun...  7.1 us
  transfers between devices with their start and end apart: 8, of which 5 were waited for; matrix products, arithmetic and copies ran while one was open for 3% of the time, Pallas kernels for 0%

profile of v1, /device:TPU:0, one launch (start us, length us, event | category | flops | bytes accessed | tf_op | source)
XLA Modules:
  0.0 174.5 jit_solution(6171661700520522014)
XLA Ops:
  0.6 0.7 convert_element_type.145
  1.4 4.9 %collective-permute-start.2 = (f32[4,256]{1,0:T(4,128)S(1)}, f32[4,256]{1,0:T(4,128)S(1)}, u32[]{:S(2)}, u32[]{:S(2)}) collective-permute-start(f32[4,256]{1,0:T(4,128)S(1)} %get-tuple-element.39), channel_id=1, source_target_pairs={{0,1},{1,2},{2,3},{4,5},{5,6},{6,7},{8,9},{9,10},{10,11},{12,13},{... | collective-permute-start | bytes 12296 | tf_op jit(solution)/shard_map/ppermute | solution.py:31
  6.3 0.0 copy-start.1
  6.3 1.3 collective-permute-start.3
  7.6 3.0 %copy.35 = bf16[144,24,256]{2,0,1:T(8,128)(2,1)S(1)} copy(f32[144,24,256]{2,1,0:T(8,128)} %param.6) | data formatting | bytes 5308416 | tf_op args[0]
  10.6 4.6 %collective-permute-start = (bf16[4,144,256]{2,1,0:T(8,128)(2,1)S(1)}, bf16[4,144,256]{2,1,0:T(8,128)(2,1)S(1)}, u32[]{:S(2)}, u32[]{:S(2)}) collective-permute-start(bf16[4,144,256]{2,1,0:T(8,128)(2,1)S(1)} %get-tuple-element.15), channel_id=1, source_target_pairs={{0,1},{1,2},{2,3},{4,5},{5,6},{6,7},{8,9},{9,10},{10,11},{12,13},{... | collective-permute-start | bytes 884744 | tf_op jit(solution)/shard_map/ppermute | solution.py:31
  15.2 1.3 collective-permute-start.1
  16.5 0.1 sine_multiply_fusion
  16.6 0.0 copy-done.1
  16.6 0.1 copy.24.refs_5_
  16.7 0.0 collective-permute-done.2
  16.7 0.0 collective-permute-done.3
  16.8 4.1 %collective-permute-done.refs_2_ = bf16[4,144,256]{2,1,0:T(8,128)(2,1)S(1)} collective-permute-done((bf16[4,144,256]{2,1,0:T(8,128)(2,1)S(1)}, bf16[4,144,256]{2,1,0:T(8,128)(2,1)S(1)}, u32[]{:S(2)}, u32[]{:S(2)}) %collective-permute-start) | collective-permute-done | bytes 294944 | tf_op jit(solution)/shard_map/ppermute | solution.py:31
  20.9 4.1 %collective-permute-done.1.refs_3_ = bf16[4,144,256]{2,1,0:T(8,128)(2,1)S(1)} collective-permute-done((bf16[4,144,256]{2,1,0:T(8,128)(2,1)S(1)}, bf16[4,144,256]{2,1,0:T(8,128)(2,1)S(1)}, u32[]{:S(2)}, u32[]{:S(2)}) %collective-permute-start.1) | collective-permute-done | bytes 294944 | tf_op jit(solution)/shard_map/ppermute | solution.py:32
  25.0 25.7 %shard_map.77 = (f32[24,144,256]{2,1,0:T(8,128)}, bf16[24,144,256]{2,1,0:T(8,128)(2,1)}) custom-call(f32[3456,256]{1,0:T(8,128)} %bitcast.43, f32[3456,256]{1,0:T(8,128)} %bitcast.44, bf16[4,144,256]{2,1,0:T(8,128)(2,1)S(1)} %collective-permute-done.refs_2_, bf16[4,144,256]{2,1,0:T(8,128)(2,1)S(1)} %collective-permute-done.1.refs_3_, ...), custom_call_target="tpu_custom_call" | custom-call | tf_op jit(solution)/shard_map/pallas_call | solution.py:105
  50.7 0.0 copy-start.2
  50.7 0.0 copy-start.3
  50.7 3.9 %all-to-all-start = ((bf16[24,144,256]{2,1,0:T(8,128)(2,1)}), bf16[24,144,256]{2,1,0:T(8,128)(2,1)S(1)}, u32[]{:S(2)}, u32[]{:S(2)}) async-start(bf16[24,144,256]{2,1,0:T(8,128)(2,1)} %get-tuple-element.7), calls=%async_computation | async-start | bytes 3538944 | tf_op jit(solution)/shard_map/all_to_all | solution.py:273
  54.6 0.0 copy-done.2
  54.6 13.5 %all_gather.7 = f32[6,32,128]{2,1,0:T(8,128)S(1)} all-gather(f32[6,8,128]{2,1,0:T(8,128)S(1)} %pad_maximum_fusion.3), channel_id=1, replica_groups=mesh['comp'=8,'band'=4] {'band'}, dimensions={1}, use_global_device_ids=true | all-gather | bytes 122880 | tf_op jit(solution)/shard_map/all_gather | solution.py:310
  68.1 0.1 fusion.158
  68.2 1.3 collective-permute-start.4
  69.5 1.3 collective-permute-start.5
  70.8 0.2 multiply_add_fusion.1
  70.9 0.2 multiply_add_fusion
  71.2 0.0 copy-done.3
  71.2 0.2 broadcast_in_dim.5.diss_ref
  71.4 0.0 collective-permute-done.4
  71.4 3.5 %collective-permute-done.5 = f32[6,32,17]{2,1,0:T(8,128)S(1)} collective-permute-done((f32[6,32,17]{2,1,0:T(8,128)S(1)}, f32[6,32,17]{2,1,0:T(8,128)S(1)}, u32[]{:S(2)}, u32[]{:S(2)}) %collective-permute-start.5) | collective-permute-done | bytes 13088 | tf_op jit(solution)/shard_map/ppermute | solution.py:32
  74.9 0.1 fusion
  75.1 0.1 copy.36
  75.2 0.1 maximum_bitcast_fusion
  75.3 0.1 fusion.8
  75.4 2.4 %all-to-all-done = bf16[24,144,256]{2,1,0:T(8,128)(2,1)S(1)} async-done(((bf16[24,144,256]{2,1,0:T(8,128)(2,1)}), bf16[24,144,256]{2,1,0:T(8,128)(2,1)S(1)}, u32[]{:S(2)}, u32[]{:S(2)}) %all-to-all-start) | async-done | bytes 1769504 | tf_op jit(solution)/shard_map/all_to_all | solution.py:273
  77.7 0.0 copy-start
  77.7 1.2 copy-done
  79.0 16.5 %shard_map.78 = (bf16[8,3,144,256]{3,2,1,0:T(8,128)(2,1)}, f32[3,8,256]{2,1,0:T(8,128)S(1)}) custom-call(bf16[8,3,144,256]{3,2,1,0:T(8,128)(2,1)} %bitcast.45, bf16[1152,1152]{1,0:T(8,128)(2,1)} %quad_ref.1, f32[1152,1]{1,0:T(8,128)S(1)} %broadcast_in_dim.5.diss_ref, f32[8,1152]{1,0:T(8,128)S(1)} %select_maximum_fusion.coef_ref), custom_call_target="tpu_custom_call" | custom-call | tf_op jit(solution)/shard_map/pallas_call | solution.py:202
  95.4 39.9 %all_gather.8 = bf16[32,3,768]{2,1,0:T(4,128)(2,1)S(1)} all-gather(bf16[1,3,768]{2,1,0:T(4,128)(2,1)S(1)} %bitcast.51), channel_id=1, replica_groups=mesh['comp'=8,'band'=4] {'band','comp'}, dimensions={0}, use_global_device_ids=true | all-gather | bytes 152064 | tf_op jit(solution)/shard_map/all_gather | solution.py:320
  135.4 0.2 reshape.276
  135.5 0.1 copy.27
  135.7 4.1 %shard_map.80 = f32[4,3,2048]{2,1,0:T(4,128)S(1)} custom-call(bf16[4,3,48,128]{3,2,1,0:T(8,128)(2,1)S(1)} %copy.29.table_ref, s32[4,3,2048]{2,1,0:T(4,128)S(1)} %bitcast.42), custom_call_target="tpu_custom_call" | custom-call | tf_op jit(solution)/shard_map/pallas_call | solution.py:249
  139.8 0.1 reshape.281
  139.9 0.1 fusion.3
  140.0 0.1 fusion.61
  140.2 0.1 fusion.14
  140.3 0.1 fusion.71
  140.4 0.1 fusion.20
  140.5 0.1 fusion.81
  140.5 0.1 fusion.26
  140.6 0.1 fusion.91
  140.7 3.6 %all-to-all-start.1 = ((bf16[24,144,256]{2,1,0:T(8,128)(2,1)}), bf16[24,144,256]{2,1,0:T(8,128)(2,1)S(1)}, u32[]{:S(2)}, u32[]{:S(2)}) async-start(bf16[24,144,256]{2,1,0:T(8,128)(2,1)} %bitcast.4), calls=%async_computation.1 | async-start | bytes 3538944 | tf_op jit(solution)/shard_map/all_to_all | solution.py:280
  144.3 0.1 fusion.32
  144.4 0.1 fusion.101
  144.5 0.1 fusion.38
  144.6 0.1 fusion.111
  144.7 0.1 fusion.44
  144.8 0.1 fusion.121
  144.9 0.1 fusion.50
  145.0 0.1 fusion.133
  145.1 0.7 fusion.143
  145.8 21.6 %all-to-all-done.1.inc_ref = bf16[24,144,256]{2,1,0:T(8,128)(2,1)S(1)} async-done(((bf16[24,144,256]{2,1,0:T(8,128)(2,1)}), bf16[24,144,256]{2,1,0:T(8,128)(2,1)S(1)}, u32[]{:S(2)}, u32[]{:S(2)}) %all-to-all-start.1) | async-done | bytes 1769504 | tf_op jit(solution)/shard_map/all_to_all | solution.py:280
  167.4 7.1 %shard_map.79 = f32[3456,256]{1,0:T(8,128)} custom-call(f32[24,144,256]{2,1,0:T(8,128)} %get-tuple-element.6.dens_ref, bf16[24,144,256]{2,1,0:T(8,128)(2,1)S(1)} %all-to-all-done.1.inc_ref), custom_call_target="tpu_custom_call" | custom-call | tf_op jit(solution)/shard_map/pallas_call | solution.py:145
  (15 shorter events, 0.2 us)
Async XLA Ops:
  1.4 15.4 %collective-permute-start.2 = (f32[4,256]{1,0:T(4,128)S(1)}, f32[4,256]{1,0:T(4,128)S(1)}, u32[]{:S(2)}, u32[]{:S(2)}) collective-permute-start(f32[4,256]{1,0:T(4,128)S(1)} %get-tuple-element.39), channel_id=1, source_target_pairs={{0,1},{1,2},{2,3},{4,5},{5,6},{6,7},{8,9},{9,10},{10,11},{12,13},{... | collective-permute-start | bytes 12296 | tf_op jit(solution)/shard_map/ppermute | solution.py:31
  6.3 10.3 %copy-start.1 = (s32[3,8,128]{2,1,0:T(8,128)S(1)}, s32[3,8,128]{2,1,0:T(8,128)}, u32[]{:S(2)}) copy-start(s32[3,8,128]{2,1,0:T(8,128)} %param.11) | copy-start | bytes 36868
  6.3 10.4 %collective-permute-start.3 = (f32[4,256]{1,0:T(4,128)S(1)}, f32[4,256]{1,0:T(4,128)S(1)}, u32[]{:S(2)}, u32[]{:S(2)}) collective-permute-start(f32[4,256]{1,0:T(4,128)S(1)} %get-tuple-element.40), channel_id=1, source_target_pairs={{1,0},{2,1},{3,2},{5,4},{6,5},{7,6},{9,8},{10,9},{11,10},{13,12},{... | collective-permute-start | bytes 12296 | tf_op jit(solution)/shard_map/ppermute | solution.py:32
  10.6 10.2 %collective-permute-start = (bf16[4,144,256]{2,1,0:T(8,128)(2,1)S(1)}, bf16[4,144,256]{2,1,0:T(8,128)(2,1)S(1)}, u32[]{:S(2)}, u32[]{:S(2)}) collective-permute-start(bf16[4,144,256]{2,1,0:T(8,128)(2,1)S(1)} %get-tuple-element.15), channel_id=1, source_target_pairs={{0,1},{1,2},{2,3},{4,5},{5,6},{6,7},{8,9},{9,10},{10,11},{12,13},{... | collective-permute-start | bytes 884744 | tf_op jit(solution)/shard_map/ppermute | solution.py:31
  15.2 9.8 %collective-permute-start.1 = (bf16[4,144,256]{2,1,0:T(8,128)(2,1)S(1)}, bf16[4,144,256]{2,1,0:T(8,128)(2,1)S(1)}, u32[]{:S(2)}, u32[]{:S(2)}) collective-permute-start(bf16[4,144,256]{2,1,0:T(8,128)(2,1)S(1)} %get-tuple-element.14), channel_id=1, source_target_pairs={{1,0},{2,1},{3,2},{5,4},{6,5},{7,6},{9,8},{10,9},{11,10},{13,12},{... | collective-permute-start | bytes 884744 | tf_op jit(solution)/shard_map/ppermute | solution.py:32
  50.7 3.9 %copy-start.2 = (f32[3,8,128]{2,1,0:T(8,128)S(1)}, f32[3,8,128]{2,1,0:T(8,128)}, u32[]{:S(2)}) copy-start(f32[3,8,128]{2,1,0:T(8,128)} %param.10) | copy-start | bytes 36868
  50.7 20.4 %copy-start.3 = (f32[1152]{0:T(1024)S(1)}, f32[1152]{0:T(1024)}, u32[]{:S(2)}) copy-start(f32[1152]{0:T(1024)} %param.9) | copy-start | bytes 13828
  50.7 27.0 %all-to-all-start = ((bf16[24,144,256]{2,1,0:T(8,128)(2,1)}), bf16[24,144,256]{2,1,0:T(8,128)(2,1)S(1)}, u32[]{:S(2)}, u32[]{:S(2)}) async-start(bf16[24,144,256]{2,1,0:T(8,128)(2,1)} %get-tuple-element.7), calls=%async_computation | async-start | bytes 3538944 | tf_op jit(solution)/shard_map/all_to_all | solution.py:273
  68.2 3.2 %collective-permute-start.4 = (f32[6,32,17]{2,1,0:T(8,128)S(1)}, f32[6,32,17]{2,1,0:T(8,128)S(1)}, u32[]{:S(2)}, u32[]{:S(2)}) collective-permute-start(f32[6,32,17]{2,1,0:T(8,128)S(1)} %get-tuple-element.21), channel_id=1, source_target_pairs={{0,4},{4,8},{8,12},{12,16},{16,20},{20,24},{24,28},{1,5},{5,9},{9,... | collective-permute-start | bytes 39176 | tf_op jit(solution)/shard_map/ppermute | solution.py:31
  69.5 5.4 %collective-permute-start.5 = (f32[6,32,17]{2,1,0:T(8,128)S(1)}, f32[6,32,17]{2,1,0:T(8,128)S(1)}, u32[]{:S(2)}, u32[]{:S(2)}) collective-permute-start(f32[6,32,17]{2,1,0:T(8,128)S(1)} %get-tuple-element.22), channel_id=1, source_target_pairs={{4,0},{8,4},{12,8},{16,12},{20,16},{24,20},{28,24},{5,1},{9,5},{13... | collective-permute-start | bytes 39176 | tf_op jit(solution)/shard_map/ppermute | solution.py:32
  77.7 1.2 copy-start
  140.7 26.7 %all-to-all-start.1 = ((bf16[24,144,256]{2,1,0:T(8,128)(2,1)}), bf16[24,144,256]{2,1,0:T(8,128)(2,1)S(1)}, u32[]{:S(2)}, u32[]{:S(2)}) async-start(bf16[24,144,256]{2,1,0:T(8,128)(2,1)} %bitcast.4), calls=%async_computation.1 | async-start | bytes 3538944 | tf_op jit(solution)/shard_map/all_to_all | solution.py:280

commit v2 on v1

--- a/solution.py
+++ b/solution.py
@@ -267,6 +267,226 @@
     return 0.5 * (extended[1:-1, 2:] - extended[1:-1, :-2])
 
 
+def coupled_kernel(sent, quad_ref, diss_ref, coef_ref, returned, table_ref, *scratch):
+    land, incs, cur, low, lines, gath = scratch[:6]
+    local_sem, push_send, push_recv, back_local, back_send, back_recv = scratch[6:12]
+    band_send, band_recv, comp_send, comp_recv = scratch[12:]
+    groups, own, count, columns = land.shape
+    total = groups * count
+    bands = gath.shape[1]
+    me = lax.axis_index("comp")
+    band = lax.axis_index("band")
+
+    def comp_copy(src, dst, send, recv, peer):
+        return pltpu.make_async_remote_copy(
+            src_ref=src,
+            dst_ref=dst,
+            send_sem=send,
+            recv_sem=recv,
+            device_id=(peer, band),
+            device_id_type=pl.DeviceIdType.MESH,
+        )
+
+    def band_copy(i, slot):
+        return pltpu.make_async_remote_copy(
+            src_ref=gath.at[me, band],
+            dst_ref=gath.at[me, slot],
+            send_sem=band_send.at[i],
+            recv_sem=band_recv.at[i],
+            device_id=(me, lax.rem(band + i, bands)),
+            device_id_type=pl.DeviceIdType.MESH,
+        )
+
+    def to_peer(i):
+        return lax.rem(me + i, groups)
+
+    def from_peer(i):
+        return lax.rem(me + groups - i, groups)
+
+    def push(j, i, slot):
+        peer = to_peer(i)
+        return comp_copy(
+            sent.at[peer * own + j], land.at[slot, j], push_send.at[j, i], push_recv.at[j, i], peer
+        )
+
+    def back(j, i, slot):
+        peer = to_peer(i)
+        return comp_copy(
+            incs.at[peer, j],
+            returned.at[slot * own + j],
+            back_send.at[j, i],
+            back_recv.at[j, i],
+            peer,
+        )
+
+    def spread(i, slot):
+        return comp_copy(gath.at[me], gath.at[slot], comp_send.at[i], comp_recv.at[i], to_peer(i))
+
+    def push_local(j):
+        return pltpu.make_async_copy(sent.at[me * own + j], land.at[me, j], local_sem.at[j])
+
+    def back_own(j):
+        return pltpu.make_async_copy(incs.at[me, j], returned.at[me * own + j], back_local.at[j])
+
+    barrier = pltpu.get_barrier_semaphore()
+
+    @pl.loop(1, groups)
+    def _(i):
+        pl.semaphore_signal(
+            barrier, inc=1, device_id=(to_peer(i), band), device_id_type=pl.DeviceIdType.MESH
+        )
+
+    @pl.loop(1, bands)
+    def _(i):
+        pl.semaphore_signal(
+            barrier,
+            inc=1,
+            device_id=(me, lax.rem(band + i, bands)),
+            device_id_type=pl.DeviceIdType.MESH,
+        )
+
+    pl.semaphore_wait(barrier, groups + bands - 2)
+
+    @pl.loop(0, own)
+    def _(j):
+        push_local(j).start()
+
+        @pl.loop(1, groups)
+        def _(i):
+            push(j, i, me).start()
+
+    tiles = 3
+    tile = total // tiles
+
+    @pl.loop(0, own)
+    def _(j):
+        push_local(j).wait()
+
+        @pl.loop(1, groups)
+        def _(i):
+            push(j, i, from_peer(i)).wait_recv()
+
+        base = land[:, j].reshape(total, columns)
+        low[0] = base
+        wide = base.astype(jnp.float32)
+        cur[...] = wide
+
+        def step(s, level):
+            after = jnp.zeros_like(level)
+            for t in range(tiles):
+                part = slice(t * tile, (t + 1) * tile)
+                product = jnp.dot(
+                    quad_ref[part, :], low[lax.rem(s, 2)], preferred_element_type=jnp.float32
+                )
+                now = cur[part, :]
+                now = now + step_source * now * (product - diss_ref[part, :] * (level / total))
+                cur[part, :] = now
+                after = after + jnp.sum(now, axis=0, keepdims=True)
+                low[lax.rem(s + 1, 2), part, :] = now.astype(jnp.bfloat16)
+            return after
+
+        lax.fori_loop(0, SRC_STEPS, step, jnp.sum(wide, axis=0, keepdims=True))
+        wide = land[:, j].reshape(total, columns).astype(jnp.float32)
+        increment = (cur[...] - wide).astype(jnp.bfloat16)
+        incs[:, j] = increment.reshape(groups, count, columns)
+        back_own(j).start()
+
+        @pl.loop(1, groups)
+        def _(i):
+            back(j, i, me).start()
+
+        lines[j] = (
+            jnp.dot(
+                coef_ref[...],
+                wide + increment.astype(jnp.float32),
+                precision=lax.Precision.HIGHEST,
+                preferred_element_type=jnp.float32,
+            )
+            / total
+        )
+
+    filled = [lines[j, 0:3] for j in range(own)]
+    filled.append(jnp.zeros((gath.shape[2] - 3 * own, columns), jnp.float32))
+    gath[me, band] = jnp.concatenate(filled, axis=0).astype(jnp.bfloat16)
+
+    @pl.loop(1, bands)
+    def _(i):
+        band_copy(i, band).start()
+
+    @pl.loop(1, bands)
+    def _(i):
+        band_copy(i, lax.rem(band + bands - i, bands)).wait_recv()
+
+    @pl.loop(1, groups)
+    def _(i):
+        spread(i, me).start()
+
+    @pl.loop(1, groups)
+    def _(i):
+        spread(i, from_peer(i)).wait_recv()
+
+    table_ref[...] = gath[...]
+
+    @pl.loop(1, bands)
+    def _(i):
+        band_copy(i, band).wait_send()
+
+    @pl.loop(1, groups)
+    def _(i):
+        spread(i, me).wait_send()
+
+    @pl.loop(0, own)
+    def _(j):
+        back_own(j).wait()
+
+        @pl.loop(1, groups)
+        def _(i):
+            push(j, i, me).wait_send()
+            back(j, i, me).wait_send()
+            back(j, i, from_peer(i)).wait_recv()
+
+
+def coupled(sent, quad_matrix, dissipation, coef, groups, bands):
+    rows, count, columns = sent.shape
+    own = rows // groups
+    total = groups * count
+    held = pl.cdiv(3 * own, 16) * 16
+    vmem = pl.BlockSpec(memory_space=pltpu.VMEM)
+    anywhere = pl.BlockSpec(memory_space=pl.ANY)
+    pair = pltpu.SemaphoreType.DMA((own, groups))
+    single = pltpu.SemaphoreType.DMA((own,))
+    return pl.pallas_call(
+        coupled_kernel,
+        in_specs=[anywhere, vmem, vmem, vmem],
+        out_specs=[anywhere, vmem],
+        out_shape=[
+            jax.ShapeDtypeStruct(sent.shape, jnp.bfloat16),
+            jax.ShapeDtypeStruct((groups, bands, held, columns), jnp.bfloat16),
+        ],
+        scratch_shapes=[
+            pltpu.VMEM((groups, own, count, columns), jnp.bfloat16),
+            pltpu.VMEM((groups, own, count, columns), jnp.bfloat16),
+            pltpu.VMEM((total, columns), jnp.float32),
+            pltpu.VMEM((2, total, columns), jnp.bfloat16),
+            pltpu.VMEM((own, coef.shape[0], columns), jnp.float32),
+            pltpu.VMEM((groups, bands, held, columns), jnp.bfloat16),
+            single,
+            pair,
+            pair,
+            single,
+            pair,
+            pair,
+            pltpu.SemaphoreType.DMA((bands,)),
+            pltpu.SemaphoreType.DMA((bands,)),
+            pltpu.SemaphoreType.DMA((groups,)),
+            pltpu.SemaphoreType.DMA((groups,)),
+        ],
+        compiler_params=pltpu.CompilerParams(
+            collective_id=0, has_side_effects=True, vmem_limit_bytes=VMEM_LIMIT
+        ),
+    )(sent, quad_matrix, dissipation[:, None], coef)
+
+
 def exchange_sources(sent, quad_matrix, dissipation, coef, groups):
     rows, count, columns = sent.shape
     own = rows // groups
@@ -315,11 +535,16 @@
     index = jnp.pad(wide[3:].astype(jnp.int32), ((0, 0), (0, 0), (0, padded_cols - wide_cols)))
     index = index.reshape(3, bands, tile_rows * padded_cols).transpose(1, 0, 2)
 
-    increment, stress = exchange_sources(sent, quad_matrix, dissipation, coef, groups)
-    own_stress = stress[:, :3].transpose(1, 0, 2).reshape(3, -1).astype(jnp.bfloat16)
-    table = lax.all_gather(own_stress, ("band", "comp"), axis=0)
-    table = table.reshape(bands, groups, 3, own_rows * columns // LANES, LANES)
-    table = table.transpose(0, 2, 1, 3, 4).reshape(bands, 3, -1, LANES)
+    if local_count % 16:
+        increment, stress = exchange_sources(sent, quad_matrix, dissipation, coef, groups)
+        own_stress = stress[:, :3].astype(jnp.bfloat16)
+        table = lax.all_gather(own_stress, "comp", axis=0)
+        table = lax.all_gather(table, "band", axis=1)
+    else:
+        increment, table = coupled(sent, quad_matrix, dissipation, coef, groups, bands)
+        table = table[:, :, : 3 * own_rows]
+    table = table.reshape(groups, bands, own_rows, 3, columns // LANES, LANES)
+    table = table.transpose(1, 3, 0, 2, 4, 5).reshape(bands, 3, -1, LANES)
     cell_stress = pick(table, index).reshape(bands, 3, tile_rows, padded_cols)
     cell_stress = cell_stress.transpose(1, 0, 2, 3).reshape(3, -1, padded_cols)[..., :wide_cols]
     new_spectrum = finish(density, increment)

time: 175 us -> 136 us (0.78)
  blocking collectives: 53.4 us -> 15 us
  Pallas kernels: 53.4 us -> 87 us
  waiting for transfers between devices: 35.7 us -> 8.93 us
  starting transfers between devices: 22.1 us -> 13.3 us
    all_gather x1 -> x0, blocking collectives: 39.9 us -> none  [on_device(): table = lax.all_gather(own_stress, ('band', 'comp'), axis=0)]
    pallas_call x1, Pallas kernels: 16.5 us -> 49.9 us  [coupled(): pl.pallas_call(coupled_kernel, in_specs=[anywhere, vmem, vmem, vmem], out...]
    all_to_all x2 -> x0, waiting for transfers between devices: 24 us -> none  [the longest x1 21.6 us: exchange_sources(): lax.all_to_all(increment.reshape(rows, count, columns), 'comp', split_axi...]
    all_to_all x2 -> x0, starting transfers between devices: 7.46 us -> none  [the longest x1 3.86 us: exchange_sources(): lax.all_to_all(sent, 'comp', split_axis=0, concat_axis=0, tiled=True)]
    ppermute x3, waiting for transfers between devices: 7.64 us -> 5.55 us  [neighbours(): after = lax.ppermute(head, axis, [(i + 1, i) for i in range(ends)])]
    unnamed x9 -> x5, local copies, waits for them, and re-layouts: 4.19 us -> 4.19 us
  transfers between devices with their start and end apart: 8 -> 6, of which waited for: 5 -> 2; matrix products, arithmetic and copies ran while one was open for 3% -> 4% of each run, Pallas kernels for 0% -> 0%
where the time goes in v2:
time: 136 us; the launch traced here: 135 us
  Pallas kernels  87 us (64%)
  blocking collectives  15 us (11%)
  starting transfers between devices  13.3 us (10%)
  waiting for transfers between devices  8.93 us (7%)
  local copies, waits for them, and re-layouts  5.14 us (4%)
  other arithmetic  4.98 us (4%)
    pallas_call x1, Pallas kernels, coupled(): pl.pallas_call(coupled_kernel, in_specs=[anywhere, vmem, vmem, vmem], out...  49.9 us
    pallas_call x1, Pallas kernels, propagate(): pl.pallas_call(functools.partial(propagate_kernel, rows), grid=grid, in_s...  25.8 us
    all_gather x1, blocking collectives, on_device(): both = lax.all_gather(both, 'band', axis=1, tiled=True)  15 us
    ppermute x3, starting transfers between devices, neighbours(): before = lax.ppermute(tail, axis, [(i, i + 1) for i in range(ends)])  9.38 us
    pallas_call x1, Pallas kernels, finish(): pl.pallas_call(functools.partial(finish_kernel, rows), grid=(pl.cdiv(coun...  7.12 us
    ppermute x3, waiting for transfers between devices, neighbours(): after = lax.ppermute(head, axis, [(i + 1, i) for i in range(ends)])  5.55 us
    unnamed x5, local copies, waits for them, and re-layouts  4.19 us
    pallas_call x1, Pallas kernels, pick(): pl.pallas_call(pick_kernel, grid=(bands,), in_specs=[pl.BlockSpec((1, 3,...  4.1 us
  transfers between devices with their start and end apart: 6, of which 2 were waited for; matrix products, arithmetic and copies ran while one was open for 4% of the time, Pallas kernels for 0%

profile of v2, /device:TPU:0, one launch (start us, length us, event | category | flops | bytes accessed | tf_op | source)
XLA Modules:
  0.0 135.3 jit_solution(6324011588012724619)
XLA Ops:
  0.6 0.7 convert_element_type.136
  1.3 0.7 pad_maximum_fusion.3
  2.0 15.0 %all_gather.3 = f32[6,32,128]{2,1,0:T(8,128)S(1)} all-gather(f32[6,8,128]{2,1,0:T(8,128)S(1)} %pad_maximum_fusion.3), channel_id=1, replica_groups=mesh['comp'=8,'band'=4] {'band'}, dimensions={1}, use_global_device_ids=true | all-gather | bytes 122880 | tf_op jit(solution)/shard_map/all_gather | solution.py:530
  17.1 0.1 fusion.158
  17.2 1.3 collective-permute-start.4
  18.5 1.3 collective-permute-start.5
  19.8 0.7 convert_element_type.131
  20.5 3.5 %collective-permute-start.2 = (f32[4,256]{1,0:T(4,128)S(1)}, f32[4,256]{1,0:T(4,128)S(1)}, u32[]{:S(2)}, u32[]{:S(2)}) collective-permute-start(f32[4,256]{1,0:T(4,128)S(1)} %get-tuple-element.39), channel_id=1, source_target_pairs={{0,1},{1,2},{2,3},{4,5},{5,6},{6,7},{8,9},{9,10},{10,11},{12,13},{... | collective-permute-start | bytes 12296 | tf_op jit(solution)/shard_map/ppermute | solution.py:31
  24.0 0.0 copy-start.1
  24.1 1.3 collective-permute-start.3
  25.4 3.0 %copy.28 = bf16[144,24,256]{2,0,1:T(8,128)(2,1)S(1)} copy(f32[144,24,256]{2,1,0:T(8,128)} %param.6) | data formatting | bytes 5308416 | tf_op args[0]
  28.4 4.6 %collective-permute-start = (bf16[4,144,256]{2,1,0:T(8,128)(2,1)S(1)}, bf16[4,144,256]{2,1,0:T(8,128)(2,1)S(1)}, u32[]{:S(2)}, u32[]{:S(2)}) collective-permute-start(bf16[4,144,256]{2,1,0:T(8,128)(2,1)S(1)} %get-tuple-element.15), channel_id=1, source_target_pairs={{0,1},{1,2},{2,3},{4,5},{5,6},{6,7},{8,9},{9,10},{10,11},{12,13},{... | collective-permute-start | bytes 884744 | tf_op jit(solution)/shard_map/ppermute | solution.py:31
  33.0 0.2 multiply_add_fusion
  33.1 0.2 multiply_add_fusion.1
  33.3 0.1 sine_multiply_fusion
  33.4 0.1 copy.18.refs_5_
  33.5 0.0 copy-done.1
  33.5 0.2 broadcast_in_dim.5.diss_ref
  33.8 0.0 collective-permute-done.2
  33.8 1.3 collective-permute-start.1
  35.1 0.0 collective-permute-done.3
  35.1 0.0 collective-permute-done.4
  35.1 0.0 collective-permute-done.5
  35.1 0.1 fusion
  35.3 0.1 copy.29
  35.4 0.1 maximum_bitcast_fusion
  35.5 0.1 fusion.8
  35.6 3.4 %collective-permute-done.refs_2_ = bf16[4,144,256]{2,1,0:T(8,128)(2,1)S(1)} collective-permute-done((bf16[4,144,256]{2,1,0:T(8,128)(2,1)S(1)}, bf16[4,144,256]{2,1,0:T(8,128)(2,1)S(1)}, u32[]{:S(2)}, u32[]{:S(2)}) %collective-permute-start) | collective-permute-done | bytes 294944 | tf_op jit(solution)/shard_map/ppermute | solution.py:31
  39.0 5.5 %collective-permute-done.1.refs_3_ = bf16[4,144,256]{2,1,0:T(8,128)(2,1)S(1)} collective-permute-done((bf16[4,144,256]{2,1,0:T(8,128)(2,1)S(1)}, bf16[4,144,256]{2,1,0:T(8,128)(2,1)S(1)}, u32[]{:S(2)}, u32[]{:S(2)}) %collective-permute-start.1) | collective-permute-done | bytes 294944 | tf_op jit(solution)/shard_map/ppermute | solution.py:32
  44.5 25.8 %shard_map.77 = (f32[24,144,256]{2,1,0:T(8,128)}, bf16[24,144,256]{2,1,0:T(8,128)(2,1)S(1)}) custom-call(f32[3456,256]{1,0:T(8,128)} %bitcast.41, f32[3456,256]{1,0:T(8,128)} %bitcast.42, bf16[4,144,256]{2,1,0:T(8,128)(2,1)S(1)} %collective-permute-done.refs_2_, bf16[4,144,256]{2,1,0:T(8,128)(2,1)S(1)} %collective-permute-done.1.refs_3_, ...), custom_call_target="tpu_custom_call" | custom-call | tf_op jit(solution)/shard_map/pallas_call | solution.py:105
  70.3 0.0 copy-start
  70.3 1.2 copy-done
  71.5 49.9 %shard_map.78 = (bf16[24,144,256]{2,1,0:T(8,128)(2,1)S(1)}, bf16[8,4,16,256]{3,2,1,0:T(8,128)(2,1)S(1)}) custom-call(bf16[24,144,256]{2,1,0:T(8,128)(2,1)} %copy-done, bf16[1152,1152]{1,0:T(8,128)(2,1)} %quad_ref.1, f32[1152,1]{1,0:T(8,128)S(1)} %broadcast_in_dim.5.diss_ref, f32[8,1152]{1,0:T(8,128)S(1)} %select_maximum_fusion.coef_ref), custom_call_target="tpu_custom_call" | custom-call | tf_op jit(solution)/shard_map/pallas_call | solution.py:458
  121.5 0.1 copy.20
  121.6 0.1 copy.21
  121.7 4.1 %shard_map.80 = f32[4,3,2048]{2,1,0:T(4,128)S(1)} custom-call(bf16[4,3,48,128]{3,2,1,0:T(8,128)(2,1)S(1)} %bitcast.38, s32[4,3,2048]{2,1,0:T(4,128)S(1)} %bitcast.39), custom_call_target="tpu_custom_call" | custom-call | tf_op jit(solution)/shard_map/pallas_call | solution.py:249
  125.8 0.1 reshape.261
  125.9 0.1 fusion.3
  126.0 0.1 fusion.61
  126.2 0.1 fusion.14
  126.2 0.1 fusion.71
  126.3 0.1 fusion.20
  126.4 0.1 fusion.81
  126.5 0.1 fusion.26
  126.6 0.1 fusion.91
  126.7 0.1 fusion.32
  126.8 0.1 fusion.101
  126.9 0.1 fusion.38
  127.0 0.1 fusion.111
  127.1 0.1 fusion.44
  127.2 0.1 fusion.121
  127.3 0.1 fusion.50
  127.4 0.1 fusion.133
  127.5 7.1 %shard_map.79 = f32[3456,256]{1,0:T(8,128)} custom-call(f32[24,144,256]{2,1,0:T(8,128)} %get-tuple-element.6.dens_ref, bf16[24,144,256]{2,1,0:T(8,128)(2,1)S(1)} %get-tuple-element.8.inc_ref), custom_call_target="tpu_custom_call" | custom-call | tf_op jit(solution)/shard_map/pallas_call | solution.py:145
  134.6 0.7 fusion.143
  (10 shorter events, 0.2 us)
Async XLA Ops:
  17.2 17.9 %collective-permute-start.4 = (f32[6,32,17]{2,1,0:T(8,128)S(1)}, f32[6,32,17]{2,1,0:T(8,128)S(1)}, u32[]{:S(2)}, u32[]{:S(2)}) collective-permute-start(f32[6,32,17]{2,1,0:T(8,128)S(1)} %get-tuple-element.21), channel_id=1, source_target_pairs={{0,4},{4,8},{8,12},{12,16},{16,20},{20,24},{24,28},{1,5},{5,9},{9,... | collective-permute-start | bytes 39176 | tf_op jit(solution)/shard_map/ppermute | solution.py:31
  18.5 16.6 %collective-permute-start.5 = (f32[6,32,17]{2,1,0:T(8,128)S(1)}, f32[6,32,17]{2,1,0:T(8,128)S(1)}, u32[]{:S(2)}, u32[]{:S(2)}) collective-permute-start(f32[6,32,17]{2,1,0:T(8,128)S(1)} %get-tuple-element.22), channel_id=1, source_target_pairs={{4,0},{8,4},{12,8},{16,12},{20,16},{24,20},{28,24},{5,1},{9,5},{13... | collective-permute-start | bytes 39176 | tf_op jit(solution)/shard_map/ppermute | solution.py:32
  20.5 13.2 %collective-permute-start.2 = (f32[4,256]{1,0:T(4,128)S(1)}, f32[4,256]{1,0:T(4,128)S(1)}, u32[]{:S(2)}, u32[]{:S(2)}) collective-permute-start(f32[4,256]{1,0:T(4,128)S(1)} %get-tuple-element.39), channel_id=1, source_target_pairs={{0,1},{1,2},{2,3},{4,5},{5,6},{6,7},{8,9},{9,10},{10,11},{12,13},{... | collective-permute-start | bytes 12296 | tf_op jit(solution)/shard_map/ppermute | solution.py:31
  24.0 9.5 %copy-start.1 = (f32[1152]{0:T(1024)S(1)}, f32[1152]{0:T(1024)}, u32[]{:S(2)}) copy-start(f32[1152]{0:T(1024)} %param.9) | copy-start | bytes 13828
  24.1 11.0 %collective-permute-start.3 = (f32[4,256]{1,0:T(4,128)S(1)}, f32[4,256]{1,0:T(4,128)S(1)}, u32[]{:S(2)}, u32[]{:S(2)}) collective-permute-start(f32[4,256]{1,0:T(4,128)S(1)} %get-tuple-element.40), channel_id=1, source_target_pairs={{1,0},{2,1},{3,2},{5,4},{6,5},{7,6},{9,8},{10,9},{11,10},{13,12},{... | collective-permute-start | bytes 12296 | tf_op jit(solution)/shard_map/ppermute | solution.py:32
  28.4 10.6 %collective-permute-start = (bf16[4,144,256]{2,1,0:T(8,128)(2,1)S(1)}, bf16[4,144,256]{2,1,0:T(8,128)(2,1)S(1)}, u32[]{:S(2)}, u32[]{:S(2)}) collective-permute-start(bf16[4,144,256]{2,1,0:T(8,128)(2,1)S(1)} %get-tuple-element.15), channel_id=1, source_target_pairs={{0,1},{1,2},{2,3},{4,5},{5,6},{6,7},{8,9},{9,10},{10,11},{12,13},{... | collective-permute-start | bytes 884744 | tf_op jit(solution)/shard_map/ppermute | solution.py:31
  33.8 10.7 %collective-permute-start.1 = (bf16[4,144,256]{2,1,0:T(8,128)(2,1)S(1)}, bf16[4,144,256]{2,1,0:T(8,128)(2,1)S(1)}, u32[]{:S(2)}, u32[]{:S(2)}) collective-permute-start(bf16[4,144,256]{2,1,0:T(8,128)(2,1)S(1)} %get-tuple-element.14), channel_id=1, source_target_pairs={{1,0},{2,1},{3,2},{5,4},{6,5},{7,6},{9,8},{10,9},{11,10},{13,12},{... | collective-permute-start | bytes 884744 | tf_op jit(solution)/shard_map/ppermute | solution.py:32
  70.3 1.2 copy-start

commit v3 on v2

--- a/solution.py
+++ b/solution.py
@@ -267,10 +267,14 @@
     return 0.5 * (extended[1:-1, 2:] - extended[1:-1, :-2])
 
 
-def coupled_kernel(sent, quad_ref, diss_ref, coef_ref, returned, table_ref, *scratch):
-    land, incs, cur, low, lines, gath = scratch[:6]
+def coupled_kernel(
+    sent, quad_ref, diss_ref, coef_ref, both_ref, returned, table_ref, state_ref, *scratch
+):
+    land, incs, cur, low, lines, gath, hold = scratch[:7]
+    scratch = scratch[1:]
     local_sem, push_send, push_recv, back_local, back_send, back_recv = scratch[6:12]
-    band_send, band_recv, comp_send, comp_recv = scratch[12:]
+    band_send, band_recv, comp_send, comp_recv = scratch[12:16]
+    tile_send, tile_recv, side_send, side_recv = scratch[16:]
     groups, own, count, columns = land.shape
     total = groups * count
     bands = gath.shape[1]
@@ -322,6 +326,22 @@
     def spread(i, slot):
         return comp_copy(gath.at[me], gath.at[slot], comp_send.at[i], comp_recv.at[i], to_peer(i))
 
+    def tile_copy(i, slot):
+        return pltpu.make_async_remote_copy(
+            src_ref=hold.at[1, band],
+            dst_ref=hold.at[1, slot],
+            send_sem=tile_send.at[i],
+            recv_sem=tile_recv.at[i],
+            device_id=(me, lax.rem(band + i, bands)),
+            device_id_type=pl.DeviceIdType.MESH,
+        )
+
+    def side_copy(k):
+        peer = to_peer(1) if k == 0 else from_peer(1)
+        return comp_copy(
+            hold.at[1], hold.at[2 * k], side_send.at[k], side_recv.at[k], peer
+        )
+
     def push_local(j):
         return pltpu.make_async_copy(sent.at[me * own + j], land.at[me, j], local_sem.at[j])
 
@@ -347,6 +367,12 @@
 
     pl.semaphore_wait(barrier, groups + bands - 2)
 
+    hold[1, band] = both_ref[...]
+
+    @pl.loop(1, bands)
+    def _(i):
+        tile_copy(i, band).start()
+
     @pl.loop(0, own)
     def _(j):
         push_local(j).start()
@@ -354,6 +380,13 @@
         @pl.loop(1, groups)
         def _(i):
             push(j, i, me).start()
+
+    @pl.loop(1, bands)
+    def _(i):
+        tile_copy(i, lax.rem(band + bands - i, bands)).wait_recv()
+
+    side_copy(0).start()
+    side_copy(1).start()
 
     tiles = 3
     tile = total // tiles
@@ -426,9 +459,13 @@
         spread(i, from_peer(i)).wait_recv()
 
     table_ref[...] = gath[...]
+    side_copy(0).wait()
+    side_copy(1).wait()
+    state_ref[...] = hold[...]
 
     @pl.loop(1, bands)
     def _(i):
+        tile_copy(i, band).wait_send()
         band_copy(i, band).wait_send()
 
     @pl.loop(1, groups)
@@ -446,7 +483,7 @@
             back(j, i, from_peer(i)).wait_recv()
 
 
-def coupled(sent, quad_matrix, dissipation, coef, groups, bands):
+def coupled(sent, quad_matrix, dissipation, coef, both, groups, bands):
     rows, count, columns = sent.shape
     own = rows // groups
     total = groups * count
@@ -457,11 +494,12 @@
     single = pltpu.SemaphoreType.DMA((own,))
     return pl.pallas_call(
         coupled_kernel,
-        in_specs=[anywhere, vmem, vmem, vmem],
-        out_specs=[anywhere, vmem],
+        in_specs=[anywhere, vmem, vmem, vmem, vmem],
+        out_specs=[anywhere, vmem, vmem],
         out_shape=[
             jax.ShapeDtypeStruct(sent.shape, jnp.bfloat16),
             jax.ShapeDtypeStruct((groups, bands, held, columns), jnp.bfloat16),
+            jax.ShapeDtypeStruct((3, bands) + both.shape, jnp.float32),
         ],
         scratch_shapes=[
             pltpu.VMEM((groups, own, count, columns), jnp.bfloat16),
@@ -470,6 +508,7 @@
             pltpu.VMEM((2, total, columns), jnp.bfloat16),
             pltpu.VMEM((own, coef.shape[0], columns), jnp.float32),
             pltpu.VMEM((groups, bands, held, columns), jnp.bfloat16),
+            pltpu.VMEM((3, bands) + both.shape, jnp.float32),
             single,
             pair,
             pair,
@@ -480,11 +519,15 @@
             pltpu.SemaphoreType.DMA((bands,)),
             pltpu.SemaphoreType.DMA((groups,)),
             pltpu.SemaphoreType.DMA((groups,)),
+            pltpu.SemaphoreType.DMA((bands,)),
+            pltpu.SemaphoreType.DMA((bands,)),
+            pltpu.SemaphoreType.DMA((2,)),
+            pltpu.SemaphoreType.DMA((2,)),
         ],
         compiler_params=pltpu.CompilerParams(
             collective_id=0, has_side_effects=True, vmem_limit_bytes=VMEM_LIMIT
         ),
-    )(sent, quad_matrix, dissipation[:, None], coef)
+    )(sent, quad_matrix, dissipation[:, None], coef, both)
 
 
 def exchange_sources(sent, quad_matrix, dissipation, coef, groups):
@@ -515,9 +558,13 @@
 
     head = spectrum[:, :SUBSTEPS].transpose(1, 0, 2).astype(jnp.bfloat16)
     tail = spectrum[:, row_count - SUBSTEPS :].transpose(1, 0, 2).astype(jnp.bfloat16)
-    before, after = neighbours(jnp.concatenate([head, tail], axis=0), "band", 0, SUBSTEPS)
+    ends = jnp.concatenate([head, tail], axis=0)
     wet = wet_mask.astype(jnp.float32)
-    wet_before, wet_after = neighbours(wet, "band", 0, SUBSTEPS)
+    wet_ends = jnp.concatenate([wet[:SUBSTEPS], wet[row_count - SUBSTEPS :]], axis=0)
+    ends = jnp.concatenate([ends, wet_ends.astype(jnp.bfloat16)[:, None]], axis=1)
+    before, after = neighbours(ends, "band", 0, SUBSTEPS)
+    wet_before = before[:, local_count].astype(jnp.float32)
+    wet_after = after[:, local_count].astype(jnp.float32)
     wet = jnp.concatenate([wet_before, wet, wet_after], axis=0)
     density, sent = propagate(
         spectrum, before, after, wet, jnp.stack([speed_x, speed_y], axis=1)
@@ -527,22 +574,25 @@
     tile_cols = circulation.shape[2]
     margin = 2 * SW_STEPS + 1
     both = jnp.concatenate([circulation, source_points.astype(jnp.float32)], axis=0)
-    both = lax.all_gather(both, "band", axis=1, tiled=True)
-    left, right = neighbours(both, "comp", 2, margin)
+    if local_count % 16:
+        increment, stress = exchange_sources(sent, quad_matrix, dissipation, coef, groups)
+        own_stress = stress[:, :3].astype(jnp.bfloat16)
+        table = lax.all_gather(own_stress, "comp", axis=0)
+        table = lax.all_gather(table, "band", axis=1)
+        both = lax.all_gather(both, "band", axis=1, tiled=True)
+        left, right = neighbours(both, "comp", 2, margin)
+    else:
+        increment, table, state = coupled(
+            sent, quad_matrix, dissipation, coef, both, groups, bands
+        )
+        table = table[:, :, : 3 * own_rows]
+        state = state.transpose(0, 2, 1, 3, 4).reshape(3, 6, bands * tile_rows, tile_cols)
+        left, both, right = state[0, ..., tile_cols - margin :], state[1], state[2, ..., :margin]
     wide = jnp.concatenate([left, both, right], axis=2)
     wide_cols = wide.shape[2]
     padded_cols = pl.cdiv(wide_cols, LANES) * LANES
     index = jnp.pad(wide[3:].astype(jnp.int32), ((0, 0), (0, 0), (0, padded_cols - wide_cols)))
     index = index.reshape(3, bands, tile_rows * padded_cols).transpose(1, 0, 2)
-
-    if local_count % 16:
-        increment, stress = exchange_sources(sent, quad_matrix, dissipation, coef, groups)
-        own_stress = stress[:, :3].astype(jnp.bfloat16)
-        table = lax.all_gather(own_stress, "comp", axis=0)
-        table = lax.all_gather(table, "band", axis=1)
-    else:
-        increment, table = coupled(sent, quad_matrix, dissipation, coef, groups, bands)
-        table = table[:, :, : 3 * own_rows]
     table = table.reshape(groups, bands, own_rows, 3, columns // LANES, LANES)
     table = table.transpose(1, 3, 0, 2, 4, 5).reshape(bands, 3, -1, LANES)
     cell_stress = pick(table, index).reshape(bands, 3, tile_rows, padded_cols)
@@ -556,7 +606,7 @@
     rimmed = jnp.pad(cell_stress * inside, ((0, 0), (1, 1), (1, 1)))
     force_down = -(diff_rows(rimmed[0]) + diff_cols(rimmed[1]))
     force_across = -(diff_rows(rimmed[1]) + diff_cols(rimmed[2]))
-    height, flow_down, flow_across = wide[0], wide[1], wide[2]
+    height, flow_down, flow_across = wide[0] * inside, wide[1] * inside, wide[2] * inside
     for repeat in range(SW_STEPS):
         down_ext = jnp.pad(flow_down, 1)
         across_ext = jnp.pad(flow_across, 1)

time: 136 us -> 112 us (0.82)
  blocking collectives: 15 us -> 0 us
  starting transfers between devices: 13.3 us -> 6.87 us
  waiting for transfers between devices: 8.93 us -> 5.42 us
  local copies, waits for them, and re-layouts: 5.14 us -> 2.67 us
  Pallas kernels: 87 us -> 89.2 us
    all_gather x1 -> x0, blocking collectives: 15 us -> none  [on_device(): both = lax.all_gather(both, 'band', axis=1, tiled=True)]
    ppermute x3 -> x1, starting transfers between devices: 9.38 us -> 5.57 us  [neighbours(): before = lax.ppermute(tail, axis, [(i, i + 1) for i in range(ends)])]
    unnamed x5 -> x8, local copies, waits for them, and re-layouts: 4.19 us -> 1.22 us
    ppermute x3 -> x1, starting transfers between devices: 3.88 us -> 1.29 us  [neighbours(): after = lax.ppermute(head, axis, [(i + 1, i) for i in range(ends)])]
    ppermute x3 -> x1, waiting for transfers between devices: 3.37 us -> 1.18 us  [neighbours(): before = lax.ppermute(tail, axis, [(i, i + 1) for i in range(ends)])]
    another operation x0 -> x1, other arithmetic: none -> 2.17 us
    pallas_call x1, Pallas kernels: 49.9 us -> 52 us  [coupled(): pl.pallas_call(coupled_kernel, in_specs=[anywhere, vmem, vmem, vmem, vmem...]
    ppermute x3 -> x1, waiting for transfers between devices: 5.55 us -> 4.24 us  [neighbours(): after = lax.ppermute(head, axis, [(i + 1, i) for i in range(ends)])]
  transfers between devices with their start and end apart: 6 -> 2, of which waited for: 2 -> 2; matrix products, arithmetic and copies ran while one was open for 4% -> 1% of each run, Pallas kernels for 0% -> 0%
where the time goes in v3:
time: 112 us; the launch traced here: 111 us
  Pallas kernels  89.2 us (80%)
  starting transfers between devices  6.87 us (6%)
  other arithmetic  6.08 us (5%)
  waiting for transfers between devices  5.42 us (5%)
  local copies, waits for them, and re-layouts  2.67 us (2%)
    pallas_call x1, Pallas kernels, coupled(): pl.pallas_call(coupled_kernel, in_specs=[anywhere, vmem, vmem, vmem, vmem...  52 us
    pallas_call x1, Pallas kernels, propagate(): pl.pallas_call(functools.partial(propagate_kernel, rows), grid=grid, in_s...  26 us
    pallas_call x1, Pallas kernels, finish(): pl.pallas_call(functools.partial(finish_kernel, rows), grid=(pl.cdiv(coun...  7.12 us
    ppermute x1, starting transfers between devices, neighbours(): before = lax.ppermute(tail, axis, [(i, i + 1) for i in range(ends)])  5.57 us
    ppermute x1, waiting for transfers between devices, neighbours(): after = lax.ppermute(head, axis, [(i + 1, i) for i in range(ends)])  4.24 us
    pallas_call x1, Pallas kernels, pick(): pl.pallas_call(pick_kernel, grid=(bands,), in_specs=[pl.BlockSpec((1, 3,...  4.1 us
  transfers between devices with their start and end apart: 2, of which 2 were waited for; matrix products, arithmetic and copies ran while one was open for 1% of the time, Pallas kernels for 0%

profile of v3, /device:TPU:0, one launch (start us, length us, event | category | flops | bytes accessed | tf_op | source)
XLA Modules:
  0.0 111.2 jit_solution(17160250011816132266)
XLA Ops:
  0.6 0.7 fusion.164
  1.4 2.2 %convert.14 = bf16[144,24,256]{2,1,0:T(8,128)(2,1)S(1)} convert(f32[144,24,256]{2,1,0:T(8,128)} %param.6) | non-fusion elementwise | flops 884736 | bytes 5308416 | tf_op jit(solution)/shard_map/convert.9
  3.6 0.0 copy-start.3
  3.6 0.2 slice_bitcast_fusion.1
  3.8 0.0 copy-start.1
  3.8 0.0 copy-start.2
  3.8 0.3 maximum_maximum_fusion
  4.1 0.2 fusion.163
  4.4 1.3 %collective-permute-start.1 = (bf16[4,145,256]{2,0,1:T(4,128)(2,1)S(1)}, bf16[4,145,256]{2,0,1:T(4,128)(2,1)S(1)}, u32[]{:S(2)}, u32[]{:S(2)}) collective-permute-start(bf16[4,145,256]{2,0,1:T(4,128)(2,1)S(1)} %get-tuple-element.18), channel_id=1, source_target_pairs={{1,0},{2,1},{3,2},{5,4},{6,5},{7,6},{9,8},{10,9},{11,10},{13,12},{... | collective-permute-start | bytes 890888 | tf_op jit(solution)/shard_map/ppermute | solution.py:32
  5.7 5.6 %collective-permute-start = (bf16[4,145,256]{2,0,1:T(4,128)(2,1)S(1)}, bf16[4,145,256]{2,0,1:T(4,128)(2,1)S(1)}, u32[]{:S(2)}, u32[]{:S(2)}) collective-permute-start(bf16[4,145,256]{2,0,1:T(4,128)(2,1)S(1)} %get-tuple-element.19), channel_id=1, source_target_pairs={{0,1},{1,2},{2,3},{4,5},{5,6},{6,7},{8,9},{9,10},{10,11},{12,13},{... | collective-permute-start | bytes 890888 | tf_op jit(solution)/shard_map/ppermute | solution.py:31
  11.2 0.2 multiply_add_fusion
  11.4 0.2 multiply_add_fusion.1
  11.6 0.1 sine_multiply_fusion
  11.7 0.1 copy.23.refs_5_
  11.8 0.0 copy-done.3
  11.8 0.2 broadcast_in_dim.6.diss_ref
  12.0 0.0 copy-done.1
  12.0 0.0 copy-done.2
  12.1 4.2 %collective-permute-done.1 = bf16[4,145,256]{2,0,1:T(4,128)(2,1)S(1)} collective-permute-done((bf16[4,145,256]{2,0,1:T(4,128)(2,1)S(1)}, bf16[4,145,256]{2,0,1:T(4,128)(2,1)S(1)}, u32[]{:S(2)}, u32[]{:S(2)}) %collective-permute-start.1) | collective-permute-done | bytes 296992 | tf_op jit(solution)/shard_map/ppermute | solution.py:32
  16.3 1.2 %collective-permute-done = bf16[4,145,256]{2,0,1:T(4,128)(2,1)S(1)} collective-permute-done((bf16[4,145,256]{2,0,1:T(4,128)(2,1)S(1)}, bf16[4,145,256]{2,0,1:T(4,128)(2,1)S(1)}, u32[]{:S(2)}, u32[]{:S(2)}) %collective-permute-start) | collective-permute-done | bytes 296992 | tf_op jit(solution)/shard_map/ppermute | solution.py:31
  17.6 26.0 %shard_map.77 = (f32[24,144,256]{2,1,0:T(8,128)}, bf16[24,144,256]{2,1,0:T(8,128)(2,1)S(1)}) custom-call(f32[3456,256]{1,0:T(8,128)} %bitcast.73, f32[3456,256]{1,0:T(8,128)} %bitcast.74, bf16[4,145,256]{2,1,0:T(8,128)(2,1)S(1)} %copy.21.refs_2_, bf16[4,145,256]{2,1,0:T(8,128)(2,1)S(1)} %copy.22.refs_3_, f32[32,256]{1,0:T(8,128)S(1)} %pad_maximum_fusion.2.refs_4_, ...), custom_call_target="tpu_custom_call" | custom-call | tf_op jit(solution)/shard_map/pallas_call | solution.py:105
  43.6 0.0 copy-start
  43.6 1.2 %copy-done = bf16[24,144,256]{2,1,0:T(8,128)(2,1)} copy-done((bf16[24,144,256]{2,1,0:T(8,128)(2,1)}, bf16[24,144,256]{2,1,0:T(8,128)(2,1)S(1)}, u32[]{:S(2)}) %copy-start) | copy-done | bytes 1769496
  44.8 52.0 %shard_map.78 = (bf16[24,144,256]{2,1,0:T(8,128)(2,1)S(1)}, bf16[8,4,16,256]{3,2,1,0:T(8,128)(2,1)S(1)}, f32[3,4,6,8,128]{4,3,2,1,0:T(8,128)S(1)}) custom-call(bf16[24,144,256]{2,1,0:T(8,128)(2,1)} %copy-done, bf16[1152,1152]{1,0:T(8,128)(2,1)} %quad_ref.1, f32[1152,1]{1,0:T(8,128)S(1)} %broadcast_in_dim.6.diss_ref, ...), custom_call_target="tpu_custom_call" | custom-call | tf_op jit(solution)/shard_map/pallas_call | solution.py:495
  96.8 0.1 slice_bitcast_fusion.3
  96.9 0.1 fusion
  97.1 0.1 copy.36
  97.2 0.1 copy.27
  97.3 0.1 copy.28
  97.4 4.1 %shard_map.80 = f32[4,3,2048]{2,1,0:T(4,128)S(1)} custom-call(bf16[4,3,48,128]{3,2,1,0:T(8,128)(2,1)S(1)} %bitcast.69, s32[4,3,2048]{2,1,0:T(4,128)S(1)} %bitcast.70), custom_call_target="tpu_custom_call" | custom-call | tf_op jit(solution)/shard_map/pallas_call | solution.py:249
  101.5 0.1 reshape.304
  101.6 0.1 fusion.142
  101.8 0.1 fusion.3
  101.9 0.1 fusion.8
  102.0 0.1 fusion.61
  102.1 0.1 fusion.14
  102.2 0.1 fusion.71
  102.3 0.1 fusion.20
  102.4 0.1 fusion.81
  102.5 0.1 fusion.26
  102.6 0.1 fusion.91
  102.7 0.1 fusion.32
  102.8 0.1 fusion.101
  102.9 0.1 fusion.38
  103.0 0.1 fusion.111
  103.1 0.1 fusion.44
  103.1 0.1 fusion.121
  103.2 0.1 fusion.50
  103.3 0.1 fusion.133
  103.4 7.1 %shard_map.79 = f32[3456,256]{1,0:T(8,128)} custom-call(f32[24,144,256]{2,1,0:T(8,128)} %get-tuple-element.7.dens_ref, bf16[24,144,256]{2,1,0:T(8,128)(2,1)S(1)} %get-tuple-element.9.inc_ref), custom_call_target="tpu_custom_call" | custom-call | tf_op jit(solution)/shard_map/pallas_call | solution.py:145
  110.6 0.7 fusion.146
  (17 shorter events, 0.2 us)
Async XLA Ops:
  3.6 8.2 %copy-start.3 = (f32[1152]{0:T(1024)S(1)}, f32[1152]{0:T(1024)}, u32[]{:S(2)}) copy-start(f32[1152]{0:T(1024)} %param.9) | copy-start | bytes 13828
  3.8 8.2 %copy-start.1 = (s32[3,8,128]{2,1,0:T(8,128)S(1)}, s32[3,8,128]{2,1,0:T(8,128)}, u32[]{:S(2)}) copy-start(s32[3,8,128]{2,1,0:T(8,128)} %param.11) | copy-start | bytes 36868
  3.8 8.2 %copy-start.2 = (f32[3,8,128]{2,1,0:T(8,128)S(1)}, f32[3,8,128]{2,1,0:T(8,128)}, u32[]{:S(2)}) copy-start(f32[3,8,128]{2,1,0:T(8,128)} %param.10) | copy-start | bytes 36868
  4.4 12.0 %collective-permute-start.1 = (bf16[4,145,256]{2,0,1:T(4,128)(2,1)S(1)}, bf16[4,145,256]{2,0,1:T(4,128)(2,1)S(1)}, u32[]{:S(2)}, u32[]{:S(2)}) collective-permute-start(bf16[4,145,256]{2,0,1:T(4,128)(2,1)S(1)} %get-tuple-element.18), channel_id=1, source_target_pairs={{1,0},{2,1},{3,2},{5,4},{6,5},{7,6},{9,8},{10,9},{11,10},{13,12},{... | collective-permute-start | bytes 890888 | tf_op jit(solution)/shard_map/ppermute | solution.py:32
  5.7 11.9 %collective-permute-start = (bf16[4,145,256]{2,0,1:T(4,128)(2,1)S(1)}, bf16[4,145,256]{2,0,1:T(4,128)(2,1)S(1)}, u32[]{:S(2)}, u32[]{:S(2)}) collective-permute-start(bf16[4,145,256]{2,0,1:T(4,128)(2,1)S(1)} %get-tuple-element.19), channel_id=1, source_target_pairs={{0,1},{1,2},{2,3},{4,5},{5,6},{6,7},{8,9},{9,10},{10,11},{12,13},{... | collective-permute-start | bytes 890888 | tf_op jit(solution)/shard_map/ppermute | solution.py:31
  43.6 1.2 %copy-start = (bf16[24,144,256]{2,1,0:T(8,128)(2,1)}, bf16[24,144,256]{2,1,0:T(8,128)(2,1)S(1)}, u32[]{:S(2)}) copy-start(bf16[24,144,256]{2,1,0:T(8,128)(2,1)S(1)} %get-tuple-element.8.sent) | copy-start | bytes 5308420

commit v4 on v3

--- a/solution.py
+++ b/solution.py
@@ -61,8 +61,8 @@
     before = before_ref[...].astype(jnp.float32)
     after = after_ref[...].astype(jnp.float32)
     total = rows + 2 * SUBSTEPS
-    for half in range(COMP_BLOCK // 8):
-        c0 = half * 8
+    halves = []
+    for c0 in range(0, COMP_BLOCK, 8):
         ax = jnp.broadcast_to(speed_ref[c0 : c0 + 8, 0:1], (8, columns))
         ay = jnp.broadcast_to(speed_ref[c0 : c0 + 8, 1:2], (8, columns))
         keep = 1.0 - jnp.abs(ax) - jnp.abs(ay)
@@ -70,16 +70,18 @@
         south = jnp.where(lane > 0, jnp.maximum(ay, 0.0), 0.0)
         north = jnp.where(lane < columns - 1, jnp.maximum(-ay, 0.0), 0.0)
         stages = [dict() for _ in range(SUBSTEPS + 1)]
-        for r in range(total):
+        halves.append((c0, keep, west, east, south, north, stages))
+    for r in range(total + SUBSTEPS):
+        for c0, keep, west, east, south, north, stages in halves:
             if r < SUBSTEPS:
                 stages[0][r] = before[r, c0 : c0 + 8]
             elif r < SUBSTEPS + rows:
                 part = pl.ds(c0 * rows + r - SUBSTEPS, 8, stride=rows)
                 stages[0][r] = jnp.concatenate([x_ref[part, :] for x_ref in x_refs], axis=1)
-            else:
+            elif r < total:
                 stages[0][r] = after[r - SUBSTEPS - rows, c0 : c0 + 8]
-            for s in range(1, SUBSTEPS + 1):
-                q = r - s
+            for s in range(SUBSTEPS, 0, -1):
+                q = r - 2 * s
                 if q < s or q >= total - s:
                     continue
                 old = stages[s - 1]

time: 112 us -> 99.4 us (0.89)
  Pallas kernels: 89.2 us -> 76.9 us
    pallas_call x1, Pallas kernels: 26 us -> 13.7 us  [propagate(): pl.pallas_call(functools.partial(propagate_kernel, rows), grid=grid, in_s...]
where the time goes in v4:
time: 99.4 us; the launch traced here: 99 us
  Pallas kernels  76.9 us (77%)
  starting transfers between devices  6.87 us (7%)
  other arithmetic  6.08 us (6%)
  waiting for transfers between devices  5.42 us (5%)
  local copies, waits for them, and re-layouts  2.67 us (3%)
  between operations  1 us (1%)
    pallas_call x1, Pallas kernels, coupled(): pl.pallas_call(coupled_kernel, in_specs=[anywhere, vmem, vmem, vmem, vmem...  52 us
    pallas_call x1, Pallas kernels, propagate(): pl.pallas_call(functools.partial(propagate_kernel, rows), grid=grid, in_s...  13.7 us
    pallas_call x1, Pallas kernels, finish(): pl.pallas_call(functools.partial(finish_kernel, rows), grid=(pl.cdiv(coun...  7.12 us
    ppermute x1, starting transfers between devices, neighbours(): before = lax.ppermute(tail, axis, [(i, i + 1) for i in range(ends)])  5.57 us
    ppermute x1, waiting for transfers between devices, neighbours(): after = lax.ppermute(head, axis, [(i + 1, i) for i in range(ends)])  4.24 us
    pallas_call x1, Pallas kernels, pick(): pl.pallas_call(pick_kernel, grid=(bands,), in_specs=[pl.BlockSpec((1, 3,...  4.1 us
    another operation x1, other arithmetic  2.17 us
  transfers between devices with their start and end apart: 2, of which 2 were waited for; matrix products, arithmetic and copies ran while one was open for 1% of the time, Pallas kernels for 0%

profile of v4, /device:TPU:0, one launch (start us, length us, event | category | flops | bytes accessed | tf_op | source)
XLA Modules:
  0.0 99.0 jit_solution(2444893310986408577)
XLA Ops:
  0.6 0.7 fusion.164
  1.4 2.2 %convert.14 = bf16[144,24,256]{2,1,0:T(8,128)(2,1)S(1)} convert(f32[144,24,256]{2,1,0:T(8,128)} %param.6) | non-fusion elementwise | flops 884736 | bytes 5308416 | tf_op jit(solution)/shard_map/convert.9
  3.6 0.0 copy-start.3
  3.6 0.2 slice_bitcast_fusion.1
  3.8 0.0 copy-start.1
  3.8 0.0 copy-start.2
  3.8 0.3 maximum_maximum_fusion
  4.1 0.2 fusion.163
  4.4 1.3 %collective-permute-start.1 = (bf16[4,145,256]{2,0,1:T(4,128)(2,1)S(1)}, bf16[4,145,256]{2,0,1:T(4,128)(2,1)S(1)}, u32[]{:S(2)}, u32[]{:S(2)}) collective-permute-start(bf16[4,145,256]{2,0,1:T(4,128)(2,1)S(1)} %get-tuple-element.18), channel_id=1, source_target_pairs={{1,0},{2,1},{3,2},{5,4},{6,5},{7,6},{9,8},{10,9},{11,10},{13,12},{... | collective-permute-start | bytes 890888 | tf_op jit(solution)/shard_map/ppermute | solution.py:32
  5.7 5.6 %collective-permute-start = (bf16[4,145,256]{2,0,1:T(4,128)(2,1)S(1)}, bf16[4,145,256]{2,0,1:T(4,128)(2,1)S(1)}, u32[]{:S(2)}, u32[]{:S(2)}) collective-permute-start(bf16[4,145,256]{2,0,1:T(4,128)(2,1)S(1)} %get-tuple-element.19), channel_id=1, source_target_pairs={{0,1},{1,2},{2,3},{4,5},{5,6},{6,7},{8,9},{9,10},{10,11},{12,13},{... | collective-permute-start | bytes 890888 | tf_op jit(solution)/shard_map/ppermute | solution.py:31
  11.2 0.2 multiply_add_fusion
  11.4 0.2 multiply_add_fusion.1
  11.6 0.1 sine_multiply_fusion
  11.7 0.1 copy.23.refs_5_
  11.8 0.0 copy-done.3
  11.8 0.2 broadcast_in_dim.6.diss_ref
  12.0 0.0 copy-done.1
  12.0 0.0 copy-done.2
  12.1 4.2 %collective-permute-done.1 = bf16[4,145,256]{2,0,1:T(4,128)(2,1)S(1)} collective-permute-done((bf16[4,145,256]{2,0,1:T(4,128)(2,1)S(1)}, bf16[4,145,256]{2,0,1:T(4,128)(2,1)S(1)}, u32[]{:S(2)}, u32[]{:S(2)}) %collective-permute-start.1) | collective-permute-done | bytes 296992 | tf_op jit(solution)/shard_map/ppermute | solution.py:32
  16.3 1.2 %collective-permute-done = bf16[4,145,256]{2,0,1:T(4,128)(2,1)S(1)} collective-permute-done((bf16[4,145,256]{2,0,1:T(4,128)(2,1)S(1)}, bf16[4,145,256]{2,0,1:T(4,128)(2,1)S(1)}, u32[]{:S(2)}, u32[]{:S(2)}) %collective-permute-start) | collective-permute-done | bytes 296992 | tf_op jit(solution)/shard_map/ppermute | solution.py:31
  17.6 13.7 %shard_map.77 = (f32[24,144,256]{2,1,0:T(8,128)}, bf16[24,144,256]{2,1,0:T(8,128)(2,1)S(1)}) custom-call(f32[3456,256]{1,0:T(8,128)} %bitcast.73, f32[3456,256]{1,0:T(8,128)} %bitcast.74, bf16[4,145,256]{2,1,0:T(8,128)(2,1)S(1)} %copy.21.refs_2_, bf16[4,145,256]{2,1,0:T(8,128)(2,1)S(1)} %copy.22.refs_3_, f32[32,256]{1,0:T(8,128)S(1)} %pad_maximum_fusion.2.refs_4_, ...), custom_call_target="tpu_custom_call" | custom-call | tf_op jit(solution)/shard_map/pallas_call | solution.py:107
  31.3 0.0 copy-start
  31.3 1.2 %copy-done = bf16[24,144,256]{2,1,0:T(8,128)(2,1)} copy-done((bf16[24,144,256]{2,1,0:T(8,128)(2,1)}, bf16[24,144,256]{2,1,0:T(8,128)(2,1)S(1)}, u32[]{:S(2)}) %copy-start) | copy-done | bytes 1769496
  32.5 52.0 %shard_map.78 = (bf16[24,144,256]{2,1,0:T(8,128)(2,1)S(1)}, bf16[8,4,16,256]{3,2,1,0:T(8,128)(2,1)S(1)}, f32[3,4,6,8,128]{4,3,2,1,0:T(8,128)S(1)}) custom-call(bf16[24,144,256]{2,1,0:T(8,128)(2,1)} %copy-done, bf16[1152,1152]{1,0:T(8,128)(2,1)} %quad_ref.1, f32[1152,1]{1,0:T(8,128)S(1)} %broadcast_in_dim.6.diss_ref, ...), custom_call_target="tpu_custom_call" | custom-call | tf_op jit(solution)/shard_map/pallas_call | solution.py:497
  84.6 0.1 slice_bitcast_fusion.3
  84.7 0.1 fusion
  84.9 0.1 copy.36
  84.9 0.1 copy.27
  85.0 0.1 copy.28
  85.2 4.1 %shard_map.80 = f32[4,3,2048]{2,1,0:T(4,128)S(1)} custom-call(bf16[4,3,48,128]{3,2,1,0:T(8,128)(2,1)S(1)} %bitcast.69, s32[4,3,2048]{2,1,0:T(4,128)S(1)} %bitcast.70), custom_call_target="tpu_custom_call" | custom-call | tf_op jit(solution)/shard_map/pallas_call | solution.py:251
  89.3 0.1 reshape.304
  89.4 0.1 fusion.142
  89.5 0.1 fusion.3
  89.6 0.1 fusion.8
  89.7 0.1 fusion.61
  89.8 0.1 fusion.14
  89.9 0.1 fusion.71
  90.0 0.1 fusion.20
  90.1 0.1 fusion.81
  90.2 0.1 fusion.26
  90.3 0.1 fusion.91
  90.4 0.1 fusion.32
  90.5 0.1 fusion.101
  90.6 0.1 fusion.38
  90.7 0.1 fusion.111
  90.8 0.1 fusion.44
  90.9 0.1 fusion.121
  91.0 0.1 fusion.50
  91.1 0.1 fusion.133
  91.2 7.1 %shard_map.79 = f32[3456,256]{1,0:T(8,128)} custom-call(f32[24,144,256]{2,1,0:T(8,128)} %get-tuple-element.7.dens_ref, bf16[24,144,256]{2,1,0:T(8,128)(2,1)S(1)} %get-tuple-element.9.inc_ref), custom_call_target="tpu_custom_call" | custom-call | tf_op jit(solution)/shard_map/pallas_call | solution.py:147
  98.3 0.7 fusion.146
  (17 shorter events, 0.2 us)
Async XLA Ops:
  3.6 8.2 %copy-start.3 = (f32[1152]{0:T(1024)S(1)}, f32[1152]{0:T(1024)}, u32[]{:S(2)}) copy-start(f32[1152]{0:T(1024)} %param.9) | copy-start | bytes 13828
  3.8 8.2 %copy-start.1 = (s32[3,8,128]{2,1,0:T(8,128)S(1)}, s32[3,8,128]{2,1,0:T(8,128)}, u32[]{:S(2)}) copy-start(s32[3,8,128]{2,1,0:T(8,128)} %param.11) | copy-start | bytes 36868
  3.8 8.2 %copy-start.2 = (f32[3,8,128]{2,1,0:T(8,128)S(1)}, f32[3,8,128]{2,1,0:T(8,128)}, u32[]{:S(2)}) copy-start(f32[3,8,128]{2,1,0:T(8,128)} %param.10) | copy-start | bytes 36868
  4.4 12.0 %collective-permute-start.1 = (bf16[4,145,256]{2,0,1:T(4,128)(2,1)S(1)}, bf16[4,145,256]{2,0,1:T(4,128)(2,1)S(1)}, u32[]{:S(2)}, u32[]{:S(2)}) collective-permute-start(bf16[4,145,256]{2,0,1:T(4,128)(2,1)S(1)} %get-tuple-element.18), channel_id=1, source_target_pairs={{1,0},{2,1},{3,2},{5,4},{6,5},{7,6},{9,8},{10,9},{11,10},{13,12},{... | collective-permute-start | bytes 890888 | tf_op jit(solution)/shard_map/ppermute | solution.py:32
  5.7 11.9 %collective-permute-start = (bf16[4,145,256]{2,0,1:T(4,128)(2,1)S(1)}, bf16[4,145,256]{2,0,1:T(4,128)(2,1)S(1)}, u32[]{:S(2)}, u32[]{:S(2)}) collective-permute-start(bf16[4,145,256]{2,0,1:T(4,128)(2,1)S(1)} %get-tuple-element.19), channel_id=1, source_target_pairs={{0,1},{1,2},{2,3},{4,5},{5,6},{6,7},{8,9},{9,10},{10,11},{12,13},{... | collective-permute-start | bytes 890888 | tf_op jit(solution)/shard_map/ppermute | solution.py:31
  31.3 1.2 %copy-start = (bf16[24,144,256]{2,1,0:T(8,128)(2,1)}, bf16[24,144,256]{2,1,0:T(8,128)(2,1)S(1)}, u32[]{:S(2)}) copy-start(bf16[24,144,256]{2,1,0:T(8,128)(2,1)S(1)} %get-tuple-element.8.sent) | copy-start | bytes 5308420

commit v5 on v4

--- a/solution.py
+++ b/solution.py
@@ -14,6 +14,7 @@
 SRC_STEPS = 4
 SW_STEPS = 8
 COMP_BLOCK = 16
+FINISH_BLOCK = 48
 LANES = 128
 VMEM_LIMIT = 50 * 1024 * 1024
 
@@ -132,7 +133,7 @@
 def finish_kernel(rows, dens_ref, inc_ref, out_ref, *parts):
     for r in range(rows):
         value = dens_ref[r] + inc_ref[r].astype(jnp.float32)
-        for c0 in range(0, COMP_BLOCK, 8):
+        for c0 in range(0, dens_ref.shape[1], 8):
             for p, part in enumerate(parts):
                 part[pl.ds(c0 * rows + r, 8, stride=rows), :] = value[
                     c0 : c0 + 8, p * LANES : (p + 1) * LANES
@@ -143,14 +144,15 @@
 
 def finish(density, increment):
     rows, count, columns = density.shape
-    spec = pl.BlockSpec((rows, COMP_BLOCK, columns), lambda i: (0, i, 0))
+    block = COMP_BLOCK if count % FINISH_BLOCK else FINISH_BLOCK
+    spec = pl.BlockSpec((rows, block, columns), lambda i: (0, i, 0))
     out = pl.pallas_call(
         functools.partial(finish_kernel, rows),
-        grid=(pl.cdiv(count, COMP_BLOCK),),
+        grid=(pl.cdiv(count, block),),
         in_specs=[spec, spec],
-        out_specs=pl.BlockSpec((COMP_BLOCK * rows, columns), lambda i: (i, 0)),
+        out_specs=pl.BlockSpec((block * rows, columns), lambda i: (i, 0)),
         out_shape=jax.ShapeDtypeStruct((count * rows, columns), jnp.float32),
-        scratch_shapes=[pltpu.VMEM((COMP_BLOCK * rows, LANES), jnp.float32)] * (columns // LANES),
+        scratch_shapes=[pltpu.VMEM((block * rows, LANES), jnp.float32)] * (columns // LANES),
         compiler_params=pltpu.CompilerParams(vmem_limit_bytes=VMEM_LIMIT),
     )(density, increment)
     return out.reshape(count, rows, columns)

time: 99.4 us -> 97.5 us (0.981)
  Pallas kernels: 76.9 us -> 75.1 us
    pallas_call x1, Pallas kernels: 7.12 us -> 5.24 us  [finish(): pl.pallas_call(functools.partial(finish_kernel, rows), grid=(pl.cdiv(coun...]
where the time goes in v5:
time: 97.5 us; the launch traced here: 97.1 us
  Pallas kernels  75.1 us (77%)
  starting transfers between devices  6.87 us (7%)
  other arithmetic  6.08 us (6%)
  waiting for transfers between devices  5.42 us (6%)
  local copies, waits for them, and re-layouts  2.67 us (3%)
  between operations  1 us (1%)
    pallas_call x1, Pallas kernels, coupled(): pl.pallas_call(coupled_kernel, in_specs=[anywhere, vmem, vmem, vmem, vmem...  52 us
    pallas_call x1, Pallas kernels, propagate(): pl.pallas_call(functools.partial(propagate_kernel, rows), grid=grid, in_s...  13.7 us
    ppermute x1, starting transfers between devices, neighbours(): before = lax.ppermute(tail, axis, [(i, i + 1) for i in range(ends)])  5.57 us
    pallas_call x1, Pallas kernels, finish(): pl.pallas_call(functools.partial(finish_kernel, rows), grid=(pl.cdiv(coun...  5.24 us
    ppermute x1, waiting for transfers between devices, neighbours(): after = lax.ppermute(head, axis, [(i + 1, i) for i in range(ends)])  4.24 us
    pallas_call x1, Pallas kernels, pick(): pl.pallas_call(pick_kernel, grid=(bands,), in_specs=[pl.BlockSpec((1, 3,...  4.1 us
    another operation x1, other arithmetic  2.17 us
  transfers between devices with their start and end apart: 2, of which 2 were waited for; matrix products, arithmetic and copies ran while one was open for 1% of the time, Pallas kernels for 0%

profile of v5, /device:TPU:0, one launch (start us, length us, event | category | flops | bytes accessed | tf_op | source)
XLA Modules:
  0.0 97.1 jit_solution(7564093441627982176)
XLA Ops:
  0.6 0.7 fusion.164
  1.4 2.2 %convert.14 = bf16[144,24,256]{2,1,0:T(8,128)(2,1)S(1)} convert(f32[144,24,256]{2,1,0:T(8,128)} %param.6) | non-fusion elementwise | flops 884736 | bytes 5308416 | tf_op jit(solution)/shard_map/convert.9
  3.6 0.0 copy-start.3
  3.6 0.2 slice_bitcast_fusion.1
  3.8 0.0 copy-start.1
  3.8 0.0 copy-start.2
  3.8 0.3 maximum_maximum_fusion
  4.1 0.2 fusion.163
  4.4 1.3 %collective-permute-start.1 = (bf16[4,145,256]{2,0,1:T(4,128)(2,1)S(1)}, bf16[4,145,256]{2,0,1:T(4,128)(2,1)S(1)}, u32[]{:S(2)}, u32[]{:S(2)}) collective-permute-start(bf16[4,145,256]{2,0,1:T(4,128)(2,1)S(1)} %get-tuple-element.18), channel_id=1, source_target_pairs={{1,0},{2,1},{3,2},{5,4},{6,5},{7,6},{9,8},{10,9},{11,10},{13,12},{... | collective-permute-start | bytes 890888 | tf_op jit(solution)/shard_map/ppermute | solution.py:33
  5.7 5.6 %collective-permute-start = (bf16[4,145,256]{2,0,1:T(4,128)(2,1)S(1)}, bf16[4,145,256]{2,0,1:T(4,128)(2,1)S(1)}, u32[]{:S(2)}, u32[]{:S(2)}) collective-permute-start(bf16[4,145,256]{2,0,1:T(4,128)(2,1)S(1)} %get-tuple-element.19), channel_id=1, source_target_pairs={{0,1},{1,2},{2,3},{4,5},{5,6},{6,7},{8,9},{9,10},{10,11},{12,13},{... | collective-permute-start | bytes 890888 | tf_op jit(solution)/shard_map/ppermute | solution.py:32
  11.2 0.2 multiply_add_fusion
  11.4 0.2 multiply_add_fusion.1
  11.6 0.1 sine_multiply_fusion
  11.7 0.1 copy.23.refs_5_
  11.8 0.0 copy-done.3
  11.8 0.2 broadcast_in_dim.6.diss_ref
  12.0 0.0 copy-done.1
  12.0 0.0 copy-done.2
  12.1 4.2 %collective-permute-done.1 = bf16[4,145,256]{2,0,1:T(4,128)(2,1)S(1)} collective-permute-done((bf16[4,145,256]{2,0,1:T(4,128)(2,1)S(1)}, bf16[4,145,256]{2,0,1:T(4,128)(2,1)S(1)}, u32[]{:S(2)}, u32[]{:S(2)}) %collective-permute-start.1) | collective-permute-done | bytes 296992 | tf_op jit(solution)/shard_map/ppermute | solution.py:33
  16.3 1.2 %collective-permute-done = bf16[4,145,256]{2,0,1:T(4,128)(2,1)S(1)} collective-permute-done((bf16[4,145,256]{2,0,1:T(4,128)(2,1)S(1)}, bf16[4,145,256]{2,0,1:T(4,128)(2,1)S(1)}, u32[]{:S(2)}, u32[]{:S(2)}) %collective-permute-start) | collective-permute-done | bytes 296992 | tf_op jit(solution)/shard_map/ppermute | solution.py:32
  17.6 13.7 %shard_map.77 = (f32[24,144,256]{2,1,0:T(8,128)}, bf16[24,144,256]{2,1,0:T(8,128)(2,1)S(1)}) custom-call(f32[3456,256]{1,0:T(8,128)} %bitcast.73, f32[3456,256]{1,0:T(8,128)} %bitcast.74, bf16[4,145,256]{2,1,0:T(8,128)(2,1)S(1)} %copy.21.refs_2_, bf16[4,145,256]{2,1,0:T(8,128)(2,1)S(1)} %copy.22.refs_3_, f32[32,256]{1,0:T(8,128)S(1)} %pad_maximum_fusion.2.refs_4_, ...), custom_call_target="tpu_custom_call" | custom-call | tf_op jit(solution)/shard_map/pallas_call | solution.py:108
  31.3 0.0 copy-start
  31.3 1.2 %copy-done = bf16[24,144,256]{2,1,0:T(8,128)(2,1)} copy-done((bf16[24,144,256]{2,1,0:T(8,128)(2,1)}, bf16[24,144,256]{2,1,0:T(8,128)(2,1)S(1)}, u32[]{:S(2)}) %copy-start) | copy-done | bytes 1769496
  32.5 52.0 %shard_map.78 = (bf16[24,144,256]{2,1,0:T(8,128)(2,1)S(1)}, bf16[8,4,16,256]{3,2,1,0:T(8,128)(2,1)S(1)}, f32[3,4,6,8,128]{4,3,2,1,0:T(8,128)S(1)}) custom-call(bf16[24,144,256]{2,1,0:T(8,128)(2,1)} %copy-done, bf16[1152,1152]{1,0:T(8,128)(2,1)} %quad_ref.1, f32[1152,1]{1,0:T(8,128)S(1)} %broadcast_in_dim.6.diss_ref, ...), custom_call_target="tpu_custom_call" | custom-call | tf_op jit(solution)/shard_map/pallas_call | solution.py:499
  84.6 0.1 slice_bitcast_fusion.3
  84.7 0.1 fusion
  84.9 0.1 copy.36
  84.9 0.1 copy.27
  85.0 0.1 copy.28
  85.2 4.1 %shard_map.80 = f32[4,3,2048]{2,1,0:T(4,128)S(1)} custom-call(bf16[4,3,48,128]{3,2,1,0:T(8,128)(2,1)S(1)} %bitcast.69, s32[4,3,2048]{2,1,0:T(4,128)S(1)} %bitcast.70), custom_call_target="tpu_custom_call" | custom-call | tf_op jit(solution)/shard_map/pallas_call | solution.py:253
  89.3 0.1 reshape.304
  89.4 0.1 fusion.142
  89.5 0.1 fusion.3
  89.6 0.1 fusion.8
  89.7 0.1 fusion.61
  89.8 0.1 fusion.14
  89.9 0.1 fusion.71
  90.0 0.1 fusion.20
  90.1 0.1 fusion.81
  90.2 0.1 fusion.26
  90.3 0.1 fusion.91
  90.4 0.1 fusion.32
  90.5 0.1 fusion.101
  90.6 0.1 fusion.38
  90.7 0.1 fusion.111
  90.8 0.1 fusion.44
  90.9 0.1 fusion.121
  91.0 0.1 fusion.50
  91.1 0.1 fusion.133
  91.2 5.2 %shard_map.79 = f32[3456,256]{1,0:T(8,128)} custom-call(f32[24,144,256]{2,1,0:T(8,128)} %get-tuple-element.7.dens_ref, bf16[24,144,256]{2,1,0:T(8,128)(2,1)S(1)} %get-tuple-element.9.inc_ref), custom_call_target="tpu_custom_call" | custom-call | tf_op jit(solution)/shard_map/pallas_call | solution.py:149
  96.4 0.7 fusion.146
  (17 shorter events, 0.2 us)
Async XLA Ops:
  3.6 8.2 %copy-start.3 = (f32[1152]{0:T(1024)S(1)}, f32[1152]{0:T(1024)}, u32[]{:S(2)}) copy-start(f32[1152]{0:T(1024)} %param.9) | copy-start | bytes 13828
  3.8 8.2 %copy-start.1 = (s32[3,8,128]{2,1,0:T(8,128)S(1)}, s32[3,8,128]{2,1,0:T(8,128)}, u32[]{:S(2)}) copy-start(s32[3,8,128]{2,1,0:T(8,128)} %param.11) | copy-start | bytes 36868
  3.8 8.2 %copy-start.2 = (f32[3,8,128]{2,1,0:T(8,128)S(1)}, f32[3,8,128]{2,1,0:T(8,128)}, u32[]{:S(2)}) copy-start(f32[3,8,128]{2,1,0:T(8,128)} %param.10) | copy-start | bytes 36868
  4.4 12.0 %collective-permute-start.1 = (bf16[4,145,256]{2,0,1:T(4,128)(2,1)S(1)}, bf16[4,145,256]{2,0,1:T(4,128)(2,1)S(1)}, u32[]{:S(2)}, u32[]{:S(2)}) collective-permute-start(bf16[4,145,256]{2,0,1:T(4,128)(2,1)S(1)} %get-tuple-element.18), channel_id=1, source_target_pairs={{1,0},{2,1},{3,2},{5,4},{6,5},{7,6},{9,8},{10,9},{11,10},{13,12},{... | collective-permute-start | bytes 890888 | tf_op jit(solution)/shard_map/ppermute | solution.py:33
  5.7 11.9 %collective-permute-start = (bf16[4,145,256]{2,0,1:T(4,128)(2,1)S(1)}, bf16[4,145,256]{2,0,1:T(4,128)(2,1)S(1)}, u32[]{:S(2)}, u32[]{:S(2)}) collective-permute-start(bf16[4,145,256]{2,0,1:T(4,128)(2,1)S(1)} %get-tuple-element.19), channel_id=1, source_target_pairs={{0,1},{1,2},{2,3},{4,5},{5,6},{6,7},{8,9},{9,10},{10,11},{12,13},{... | collective-permute-start | bytes 890888 | tf_op jit(solution)/shard_map/ppermute | solution.py:32
  31.3 1.2 %copy-start = (bf16[24,144,256]{2,1,0:T(8,128)(2,1)}, bf16[24,144,256]{2,1,0:T(8,128)(2,1)S(1)}, u32[]{:S(2)}) copy-start(bf16[24,144,256]{2,1,0:T(8,128)(2,1)S(1)} %get-tuple-element.8.sent) | copy-start | bytes 5308420
